TPU v7x, 256 devices: a whole 4x4x8 slice. The times are simulated.
256 devices in a mesh: outer: 64 (over y, x_lo, z), inner: 4 (over x_hi, core).
Axes of the slice: x: 4 (x_hi: 2, x_lo: 2; x = x_hi * 2 + x_lo), y: 4, z: 8, core: 2. Of those that a mesh axis runs over, the one named last changes fastest.
Arguments:
- queries: bfloat16 [4, 8192, 1024], P('inner', 'outer'), may hold values from -120 to 120
- keys: bfloat16 [4, 8192, 128], P('inner', 'outer'), may hold values from -4.5 to 4.5
- values: bfloat16 [4, 8192, 128], P('inner', 'outer'), may hold values from -5 to 5
- grad_out: bfloat16 [4, 8192, 1024], P('inner', 'outer'), may hold values from -5 to 5
- block_pos: int32 [4, 128], replicated, may hold values from 0 to 255, as said below
Outputs:
- attended: bfloat16 [4, 8192, 1024], P('inner', 'outer')
- query_grad: bfloat16 [4, 8192, 1024], P('inner', 'outer')
- key_grad: bfloat16 [4, 8192, 128], P('inner', 'outer')
- value_grad: bfloat16 [4, 8192, 128], P('inner', 'outer')
Inputs may be any that keep to these rules, and one draw needn't show every extreme that they name: `block_pos`: for each sequence s, rows 2s and 2s+1 together hold each block number once. In each column pair 2o, 2o+1 of a row the first entry b is below 128 and the second is 255 - b.
All inputs are finite; a program needn't handle non-finite values.
Results may differ from a plain program's by a relative error of at most 0.035.
Values may be sent and summed in bfloat16 or wider, within the bound.
A program may use at most 128 MiB of HBM per device.

v0:
```python
import jax
import jax.numpy as jnp
from jax import lax
from jax.sharding import PartitionSpec as P

NEG_FILL = -1e30


def from_partner(block, axis, distance):
    count = lax.axis_size(axis)
    route = []
    for low in range(count):
        high = low | 1 << distance
        if high != low and high < count:
            route += [(low, high), (high, low)]
    return lax.ppermute(block, axis, route)


def dot_rows(left, right):
    return lax.dot_general(
        left, right, (((1,), (1,)), ((), ())), preferred_element_type=jnp.float32
    )


def dot_cols(left, right):
    return lax.dot_general(
        left, right, (((0,), (0,)), ((), ())), preferred_element_type=jnp.float32
    )


def block_count(key_places, query_places, width_keys):
    visible = jnp.sum((key_places <= jnp.max(query_places)).astype(jnp.int32))
    return (visible + width_keys - 1) // width_keys


def attend_forward(
    query_rows, query_places, key_sorted, value_sorted, key_places, width_keys, blocks, score_scale
):
    row_count = query_rows.shape[0]

    def advance(block_index, carried):
        maxima, totals, weighted = carried
        start = block_index * width_keys
        key_block = lax.dynamic_slice_in_dim(key_sorted, start, width_keys, 0)
        value_block = lax.dynamic_slice_in_dim(value_sorted, start, width_keys, 0)
        place_block = lax.dynamic_slice_in_dim(key_places, start, width_keys, 0)
        scores = dot_rows(query_rows, key_block) * score_scale
        visible = place_block[None, :] <= query_places[:, None]
        scores = jnp.where(visible, scores, NEG_FILL)
        new_max = jnp.maximum(maxima, jnp.max(scores, axis=1))
        factor = jnp.exp(maxima - new_max)
        weights = jnp.where(visible, jnp.exp(scores - new_max[:, None]), 0.0)
        totals = totals * factor + jnp.sum(weights, axis=1)
        weighted = weighted * factor[:, None] + jnp.dot(
            weights.astype(jnp.bfloat16), value_block, preferred_element_type=jnp.float32
        )
        return (new_max, totals, weighted)

    initial = (
        jnp.full((row_count,), NEG_FILL, jnp.float32),
        jnp.zeros((row_count,), jnp.float32),
        jnp.zeros((row_count, value_sorted.shape[1]), jnp.float32),
    )
    return lax.fori_loop(0, blocks, advance, initial)


def attend_backward(
    query_rows,
    grad_rows,
    log_totals,
    deltas,
    query_places,
    key_sorted,
    value_sorted,
    key_places,
    width_keys,
    blocks,
    score_scale,
    grads_sorted,
):

    def advance(block_index, carried):
        query_grad, grads_now = carried
        start = block_index * width_keys
        key_block = lax.dynamic_slice_in_dim(key_sorted, start, width_keys, 0)
        value_block = lax.dynamic_slice_in_dim(value_sorted, start, width_keys, 0)
        place_block = lax.dynamic_slice_in_dim(key_places, start, width_keys, 0)
        scores = dot_rows(query_rows, key_block) * score_scale
        visible = place_block[None, :] <= query_places[:, None]
        probs = jnp.where(
            visible, jnp.exp(jnp.where(visible, scores, NEG_FILL) - log_totals[:, None]), 0.0
        )
        grad_probs = dot_rows(grad_rows, value_block)
        grad_scores = (probs * (grad_probs - deltas[:, None])).astype(jnp.bfloat16)
        query_grad = query_grad + jnp.dot(
            grad_scores, key_block, preferred_element_type=jnp.float32
        )
        key_part = dot_cols(grad_scores, query_rows)
        value_part = dot_cols(probs.astype(jnp.bfloat16), grad_rows)
        previous = lax.dynamic_slice_in_dim(grads_now, start, width_keys, 0)
        grads_now = lax.dynamic_update_slice_in_dim(
            grads_now, previous + jnp.concatenate([key_part, value_part], axis=1), start, 0
        )
        return (query_grad, grads_now)

    initial = (jnp.zeros(query_rows.shape, jnp.float32), grads_sorted)
    return lax.fori_loop(0, blocks, advance, initial)


def body(queries, keys, values, grad_out, block_pos):
    tok_count = queries.shape[1]
    width = queries.shape[2]
    head_dim = keys.shape[2]
    head_count = width // head_dim
    half_block = tok_count // 2
    group_size = half_block * head_count
    score_scale = head_dim ** (-0.5)
    outer_size = lax.axis_size("outer")
    outer_index = lax.axis_index("outer")
    inner_index = lax.axis_index("inner")
    is_even = inner_index % 2 == 0
    local_queries = queries[0]
    local_grads = grad_out[0]
    local_kv = jnp.concatenate([keys[0], values[0]], axis=1)
    offsets = jnp.arange(half_block, dtype=jnp.int32)

    def group_places(half_index, slot):
        first_block = block_pos[half_index, 2 * outer_index + slot]
        return jnp.repeat(first_block * half_block + offsets, head_count)

    def group_rows(source, slot):
        return source[slot * half_block : (slot + 1) * half_block].reshape(group_size, head_dim)

    query_groups = [
        (
            group_rows(local_queries, slot),
            group_rows(local_grads, slot),
            group_places(inner_index, slot),
        )
        for slot in (0, 1)
    ]
    partner_kv = from_partner(local_kv, "inner", 0)
    lower_kv = jnp.where(is_even, local_kv, partner_kv)
    upper_kv = jnp.where(is_even, partner_kv, local_kv)
    windows = lax.all_gather(
        jnp.concatenate([lower_kv, upper_kv], axis=0), "outer", axis=0, tiled=True
    )
    first_half = inner_index - inner_index % 2
    table = lax.dynamic_slice_in_dim(block_pos, first_half, 2, 0)
    table = table.reshape(2, outer_size, 2).transpose(1, 0, 2)
    key_places = (table[..., None] * half_block + offsets).reshape(-1)
    key_order = jnp.argsort(key_places)
    sorted_kv = windows[key_order]
    sorted_places = key_places[key_order]
    key_sorted = sorted_kv[:, :head_dim]
    value_sorted = sorted_kv[:, head_dim:]
    key_total = windows.shape[0]
    per_device = key_total // outer_size
    shards_each = max(1, 512 // per_device)
    while outer_size % shards_each:
        shards_each = shards_each // 2
    width_keys = per_device * shards_each
    unit_groups = [[number] for number in range(len(query_groups))]
    states = [None] * len(query_groups)
    for unit, members in zip(query_groups, unit_groups):
        blocks = block_count(sorted_places, unit[2], width_keys)
        maxima, totals, weighted = attend_forward(
            unit[0],
            unit[2],
            key_sorted,
            value_sorted,
            sorted_places,
            width_keys,
            blocks,
            score_scale,
        )
        for position, number in enumerate(members):
            states[number] = (maxima, totals, weighted)
    own_states = states[:2]
    attended_groups = []
    log_list = []
    delta_list = []
    for slot in (0, 1):
        maxima, totals, weighted = own_states[slot]
        attended_rows = (weighted / totals[:, None]).astype(jnp.bfloat16)
        attended_groups.append(attended_rows)
        log_list.append(maxima + jnp.log(totals))
        delta_list.append(
            jnp.sum(
                query_groups[slot][1].astype(jnp.float32) * attended_rows.astype(jnp.float32),
                axis=1,
            )
        )
    attended = jnp.concatenate(
        [rows.reshape(half_block, width) for rows in attended_groups], axis=0
    )[None]
    back_units = [
        (entry[0], entry[1], log_list[number], delta_list[number], entry[2])
        for number, entry in enumerate(query_groups)
    ]
    grads_sorted = jnp.zeros((key_total, 2 * head_dim), jnp.float32)
    query_grads = [None] * len(query_groups)
    for unit, members in zip(back_units, unit_groups):
        blocks = block_count(sorted_places, unit[4], width_keys)
        unit_grad, grads_sorted = attend_backward(
            unit[0],
            unit[1],
            unit[2],
            unit[3],
            unit[4],
            key_sorted,
            value_sorted,
            sorted_places,
            width_keys,
            blocks,
            score_scale,
            grads_sorted,
        )
        for position, number in enumerate(members):
            query_grads[number] = unit_grad
    own_grads = query_grads[:2]
    query_grad = jnp.concatenate(
        [
            (rows * score_scale).astype(jnp.bfloat16).reshape(half_block, width)
            for rows in own_grads
        ],
        axis=0,
    )[None]
    grads_storage = jnp.zeros_like(grads_sorted).at[key_order].set(grads_sorted)
    summed = lax.psum_scatter(grads_storage, "outer", scatter_dimension=0, tiled=True)
    mine = jnp.where(is_even, summed[:tok_count], summed[tok_count:])
    theirs = jnp.where(is_even, summed[tok_count:], summed[:tok_count])
    combined = mine + from_partner(theirs.astype(jnp.bfloat16), "inner", 0).astype(theirs.dtype)
    key_grad = (combined[:, :head_dim] * score_scale).astype(jnp.bfloat16)[None]
    value_grad = combined[:, head_dim:].astype(jnp.bfloat16)[None]
    return (attended, query_grad, key_grad, value_grad)


def solution(mesh):
    return jax.shard_map(
        body,
        mesh=mesh,
        in_specs=(
            P("inner", "outer", None),
            P("inner", "outer", None),
            P("inner", "outer", None),
            P("inner", "outer", None),
            P(),
        ),
        out_specs=(
            P("inner", "outer", None),
            P("inner", "outer", None),
            P("inner", "outer", None),
            P("inner", "outer", None),
        ),
        check_vma=False,
    )
```

profile of v0, /device:TPU:4, one launch (start us, length us, event | category | flops | bytes accessed | tf_op | source)
XLA Modules:
  0.0 1182.9 jit_solution(14523851611131540543)
XLA Ops:
  14.8 7.8 sort.17
  22.6 90.5 %gather_fusion = s32[16384]{0:T(1024)S(1)} fusion(s32[16384]{0:T(1024)S(1)} %add.145, s32[16384]{0:T(1024)S(1)} %get-tuple-element.505), kind=kCustom, calls=%fused_computation | custom fusion | bytes 196608 | tf_op jit(solution)/shard_map/gather | solution.py:154
  113.8 2.0 convert_reduce_fusion.1
  117.3 207.9 %all-gather.2.cloned.1.call-done = bf16[16384,256]{1,0:T(8,128)(2,1)} async-done(((bf16[256,256]{1,0:T(8,128)(2,1)}), bf16[16384,256]{1,0:T(8,128)(2,1)}) %all-gather.2.cloned.1.call-update) | async-done | bytes 8388624 | tf_op jit(solution)/shard_map/all_gather | solution.py:145
  325.2 65.2 %gather_fusion.1 = bf16[16384,256]{1,0:T(8,128)(2,1)} fusion(bf16[16384,256]{1,0:T(8,128)(2,1)} %all-gather.2.cloned.1.call-done, s32[16384]{0:T(1024)S(1)} %get-tuple-element.505), kind=kCustom, calls=%fused_computation.1 | custom fusion | bytes 16842752 | tf_op jit(solution)/shard_map/gather | solution.py:153
  390.5 5.7 fusion.77
  396.2 9.7 while.56
  406.0 96.9 %while.57 = (s32[]{:T(128)}, f32[512]{0:T(512)S(1)}, f32[512]{0:T(512)S(1)}, f32[512,128]{1,0:T(8,128)S(1)}, s32[]{:T(128)}, /*index=5*/s32[16384]{0:T(1024)S(1)...) while((s32[]{:T(128)}, f32[512]{0:T(512)S(1)}, ...), condition=%wide.region_12.13_spmd.clone, body=%wide.region_9.12_spmd.clone.sunk | while | flops 137495552 | bytes 4118975 | solution.py:64
  430.5 1.4 convolution_add_fusion.9
  503.2 7.7 broadcast.73.clone
  510.9 19.9 %while.58 = (s32[]{:T(128)}, f32[512,128]{1,0:T(8,128)S(1)}, f32[16384,256]{0,1:T(8,128)}, s32[]{:T(128)}, s32[16384]{0:T(1024)S(1)}, /*index=5*/bf16[16384,128]...) while((s32[]{:T(128)}, f32[512,128]{1,0:T(8,128)S(1)}, ...), condition=%wide.region_15.16_spmd.clone, body=%wide.region_14.15_spmd.clone.sunk | while | flops 338231296 | bytes 8276439 | solution.py:107
  515.6 1.9 fusion.161
  522.2 1.9 fusion.161
  528.8 1.9 fusion.161
  531.0 198.8 %while.59 = (s32[]{:T(128)}, f32[512,128]{1,0:T(8,128)S(1)}, f32[16384,256]{0,1:T(8,128)}, s32[]{:T(128)}, s32[16384]{0:T(1024)S(1)}, /*index=5*/bf16[16384,128]...) while((s32[]{:T(128)}, f32[512,128]{1,0:T(8,128)S(1)}, ...), condition=%wide.region_18.19_spmd.clone, body=%wide.region_17.18_spmd.clone.sunk | while | flops 338231296 | bytes 8276439 | solution.py:107
  535.7 1.9 fusion.176
  542.3 1.9 fusion.176
  549.0 1.9 fusion.176
  555.6 1.9 fusion.176
  562.2 1.9 fusion.176
  568.8 1.9 fusion.176
  575.4 1.9 fusion.176
  582.0 1.9 fusion.176
  588.6 1.9 fusion.176
  595.3 1.9 fusion.176
  601.9 1.9 fusion.176
  608.5 1.9 fusion.176
  615.1 1.9 fusion.176
  621.8 1.9 fusion.176
  628.4 1.9 fusion.176
  635.1 1.9 fusion.176
  641.7 1.9 fusion.176
  648.3 1.9 fusion.176
  655.0 1.9 fusion.176
  661.6 1.9 fusion.176
  668.3 1.9 fusion.176
  674.9 1.9 fusion.176
  681.5 2.0 fusion.176
  688.1 1.9 fusion.176
  694.8 1.9 fusion.176
  701.4 1.9 fusion.176
  708.0 1.9 fusion.176
  714.6 1.9 fusion.176
  721.3 1.9 fusion.176
  727.9 1.9 fusion.176
  729.8 17.5 %copy.17 = f32[16384,256]{1,0:T(8,128)} copy(f32[16384,256]{0,1:T(8,128)} %get-tuple-element.253) | data formatting | bytes 33554432 | tf_op jit(solution)/shard_map/while | solution.py:107
  747.3 74.8 %scatter_custom_fusion = f32[16384,256]{1,0:T(8,128)} fusion(s32[16384]{0:T(1024)S(1)} %get-tuple-element.504, f32[16384,256]{1,0:T(8,128)} %copy.17, f32[]{:T(128)} %constant.125.clone.1), kind=kCustom, calls=%fused_computation.85 | custom fusion | bytes 16777728 | tf_op jit(solution)/shard_map/scatter | solution.py:229
  823.2 348.3 %reduce-scatter.2.cloned.1.call-done = f32[256,256]{1,0:T(8,128)} async-done(((f32[16384,256]{1,0:T(8,128)}), f32[256,256]{1,0:T(8,128)}) %reduce-scatter.2.cloned.1.call-update) | async-done | bytes 262160 | tf_op jit(solution)/shard_map/reduce_scatter | solution.py:230
  (616 shorter events, 270.6 us)
Async XLA Ops:
  7.2 318.1 %all-gather.2.cloned.1.call-start = ((), (), s32[]{:S(2)}) async-start(), calls=%async_computation.1 | async-start | bytes 8519680 | tf_op jit(solution)/shard_map/all_gather | solution.py:145
  8.0 1.3 collective-permute-start
  10.8 1160.6 %reduce-scatter.2.cloned.1.call-start = ((), (), s32[]{:S(2)}) async-start(), calls=%async_computation.2 | async-start | bytes 17039360 | tf_op jit(solution)/shard_map/reduce_scatter | solution.py:230
  22.6 94.4 %copy-start = (bf16[1,128,1024]{2,1,0:T(8,128)(2,1)S(1)}, bf16[1,128,1024]{2,1,0:T(8,128)(2,1)}, u32[]{:S(2)}) copy-start(bf16[1,128,1024]{2,1,0:T(8,128)(2,1)} %param.13) | copy-start | bytes 786436
  22.6 94.6 %copy-start.1 = (bf16[1,128,1024]{2,1,0:T(8,128)(2,1)S(1)}, bf16[1,128,1024]{2,1,0:T(8,128)(2,1)}, u32[]{:S(2)}) copy-start(bf16[1,128,1024]{2,1,0:T(8,128)(2,1)} %param.16) | copy-start | bytes 786436
  1172.4 1.3 collective-permute-start.1
Sparse Core Ops, SparseCore 0:
  10.9 314.2 all-gather.1
  822.2 349.1 reduce-scatter.1
where the time goes:
time: 1190 us; the launch traced here: 1180 us
  waiting for transfers between devices  558 us (47%)
  local copies, waits for them, and re-layouts  280 us (24%)
  matrix products  234 us (20%)
  other arithmetic  90.1 us (8%)
  between operations  16.9 us (1%)
    reduce_scatter x1, waiting for transfers between devices, body(): lax.psum_scatter(grads_storage, 'outer', scatter_dimension=0, tiled=True)  348 us
    all_gather x1, waiting for transfers between devices, body(): lax.all_gather(jnp.concatenate([lower_kv, upper_kv], axis=0), 'outer', ax...  208 us
    dot_general x99, matrix products, dot_rows(): lax.dot_general(left, right, (((1,), (1,)), ((), ())), preferred_element_...  124 us
    gather x1, local copies, waits for them, and re-layouts, body(): sorted_places = key_places[key_order]  90.5 us
    scatter x1, local copies, waits for them, and re-layouts, body(): grads_storage = jnp.zeros_like(grads_sorted).at[key_order].set(grads_sorted)  74.8 us
    gather x1, local copies, waits for them, and re-layouts, body(): sorted_kv = windows[key_order]  65.2 us
    dynamic_update_slice x33, other arithmetic, advance(): lax.dynamic_update_slice_in_dim(grads_now, previous + jnp.concatenate([ke...  63.5 us
    dot_general x33, matrix products, advance(): jnp.dot(weights.astype(jnp.bfloat16), value_block, preferred_element_type...  47.6 us
  transfers between devices with their start and end apart: 4, of which 4 were waited for; matrix products, arithmetic and copies ran while one was open for 9% of the time, Pallas kernels for 0%

commit v1 on v0

v1 whole, which is shorter than its diff:
```python
import jax
import jax.numpy as jnp
from jax import lax
from jax.experimental import pallas as pl
from jax.experimental.pallas import tpu as pltpu
from jax.sharding import PartitionSpec as P

MESH = pl.DeviceIdType.MESH
NEG = -1e30
BIG = 1e30
BLK = 64
DIM = 128
HEADS = 8
ROWS = BLK * HEADS
CHUNKS = 16
SCALE = DIM**-0.5
C2 = SCALE * 1.4426950408889634

YORDER = (0, -1, 1, 2)
NEAR = (0, -1, 1, -2)
FAR = (2, -3, 3, 4)


def a_chunk(dz):
    return [(0, dy, dz) for dy in YORDER]


def b_chunk(dy, part):
    return [(1, dy, dz) for dz in part]


TABLE = [
    a_chunk(0),
    a_chunk(-1),
    a_chunk(1),
    b_chunk(0, NEAR),
    b_chunk(0, FAR),
    b_chunk(-1, NEAR),
    b_chunk(1, NEAR),
    a_chunk(-2),
    a_chunk(2),
    b_chunk(-1, FAR),
    b_chunk(1, FAR),
    a_chunk(-3),
    a_chunk(3),
    b_chunk(2, NEAR),
    b_chunk(2, FAR),
    a_chunk(4),
]


def nt(a, b):
    return lax.dot_general(a, b, (((1,), (0,)), ((), ())), preferred_element_type=jnp.float32)


def tn(a, b):
    return lax.dot_general(a, b, (((0,), (0,)), ((), ())), preferred_element_type=jnp.float32)


def row_sum(x):
    return jnp.sum(x, axis=0, keepdims=True)


def row_max(x):
    return jnp.max(x, axis=0, keepdims=True)


def kernel(
    pos,
    q_ref,
    k_ref,
    v_ref,
    g_ref,
    att_ref,
    dq_ref,
    dk_ref,
    dv_ref,
    buf,
    own,
    pq,
    pg,
    qn,
    gn,
    qt,
    gt,
    ot,
    dqt,
    stat,
    pstat,
    lse,
    pot,
    pdq,
    tf,
    snd,
    r1,
    r2,
    sy,
    ry,
    sz,
    rz,
    xs,
    rx,
    dg,
    kt,
    lsem,
    ssem,
    rsem,
):
    outer = lax.axis_index("outer")
    inner = lax.axis_index("inner")
    yy = outer // 16
    xx = (outer // 8) % 2
    zz = outer % 8
    mate = inner + 1 - 2 * (inner % 2)

    def at(x, dy, dz):
        return (((yy + dy + 4) % 4) * 2 + x) * 8 + (zz + dz + 8) % 8

    yp, ym = (at(xx, 1, 0), inner), (at(xx, -1, 0), inner)
    zp, zm = (at(xx, 0, 1), inner), (at(xx, 0, -1), inner)
    xp = (at(1 - xx, 0, 0), inner)
    cp = (outer, mate)

    barrier = pltpu.get_barrier_semaphore()
    for dev in (yp, ym, zp, zm, xp, cp):
        pl.semaphore_signal(barrier, inc=1, device_id=dev, device_id_type=MESH)

    for w, k in enumerate((k_ref, v_ref)):
        own[2 * w] = k[0:BLK, :]
        own[2 * w + 1] = k[BLK : 2 * BLK, :]
    pl.semaphore_wait(barrier, 6)

    msgs = {}

    def msg(name, src, dst, dev):
        at_sem = len(msgs)
        msgs[name] = pltpu.make_async_remote_copy(
            src_ref=src,
            dst_ref=dst,
            send_sem=ssem.at[at_sem],
            recv_sem=rsem.at[at_sem],
            device_id=dev,
            device_id_type=MESH,
        )

    def go(*names):
        for name in names:
            msgs[name].start()

    def got(*names):
        for name in names:
            msgs[name].wait_recv()

    msg("x", own, buf.at[3 * xx, 0], xp)
    msg("q", q_ref, pq, cp)
    msg("g", g_ref, pg, cp)
    msg("ay1", buf.at[0, 0], buf.at[0, 1], yp)
    msg("ay2", buf.at[0, 0], buf.at[0, 2], ym)
    msg("ay3", buf.at[0, 1], buf.at[0, 3], yp)
    for w in range(4):
        msg("azp%d" % w, buf.at[0, w], buf.at[1, w], zp)
        msg("azm%d" % w, buf.at[0, w], buf.at[2, w], zm)
        msg("byp%d" % w, buf.at[3, w], buf.at[5, w], yp)
        msg("bym%d" % w, buf.at[3, w], buf.at[6, w], ym)
    msg("a7", buf.at[1], buf.at[7], zp)
    msg("a8", buf.at[2], buf.at[8], zm)
    msg("a11", buf.at[7], buf.at[11], zp)
    msg("a12", buf.at[8], buf.at[12], zm)
    msg("a15p", buf.at[11, pl.ds(0, 2)], buf.at[15, pl.ds(0, 2)], zp)
    msg("a15m", buf.at[12, pl.ds(2, 2)], buf.at[15, pl.ds(2, 2)], zm)
    msg("bz1", buf.at[3, 0], buf.at[3, 1], zp)
    msg("bz2", buf.at[3, 0], buf.at[3, 2], zm)
    msg("bz3", buf.at[3, 1], buf.at[3, 3], zp)
    msg("bz4", buf.at[3, 2], buf.at[4, 0], zm)
    msg("bz5", buf.at[3, 3], buf.at[4, 1], zp)
    msg("bz6", buf.at[4, 0], buf.at[4, 2], zm)
    msg("bz7", buf.at[4, 1], buf.at[4, 3], zp)
    msg("b9", buf.at[4], buf.at[9], yp)
    msg("b10", buf.at[4], buf.at[10], ym)
    msg("b13", buf.at[5], buf.at[13], yp)
    msg("b14", buf.at[10], buf.at[14], ym)
    msg("stat", stat, pstat, cp)
    msg("ot", ot.at[1], pot, cp)
    msg("dq", dqt.at[1], pdq, cp)
    msg("r15m", snd.at[15, pl.ds(0, 2)], r1.at[11, pl.ds(0, 2)], zm)
    msg("r15p", snd.at[15, pl.ds(2, 2)], r1.at[12, pl.ds(2, 2)], zp)
    msg("r11", snd.at[11], r1.at[7], zm)
    msg("r12", snd.at[12], r1.at[8], zp)
    msg("r7", snd.at[7], r1.at[1], zm)
    msg("r8", snd.at[8], r1.at[2], zp)
    msg("r1", snd.at[1], r1.at[0], zm)
    msg("r2", snd.at[2], r2.at[0], zp)
    msg("r13", snd.at[13], r1.at[5], ym)
    msg("r14", snd.at[14], r1.at[10], yp)
    msg("r5", snd.at[5], r1.at[3], ym)
    msg("r9", snd.at[9], r1.at[4], ym)
    msg("r6", snd.at[6], r2.at[1], yp)
    msg("r10", snd.at[10], r2.at[2], yp)
    for n, dev in enumerate((ym, ym, yp)):
        msg("ry%d" % n, sy.at[n], ry.at[n], dev)
    for n, dev in enumerate((zm, zm, zm, zm, zp, zp, zp)):
        msg("rz%d" % n, sz.at[n], rz.at[n], dev)
    msg("rx", xs, rx, xp)

    go("x", "q", "g")
    local = pltpu.make_async_copy(own, buf.at[3 * xx, 0], lsem)
    local.start()

    ql = [pos[inner, 2 * outer], pos[mate, 2 * outer]]
    for c in range(CHUNKS):
        for w in range(4):
            t, dy, dz = TABLE[c][w]
            kt[4 * c + w] = pos[inner, 2 * at(t, dy, dz)]

    def spread(p, src, rows, cols):
        for h in range(HEADS):
            lanes = slice(h * DIM, (h + 1) * DIM)
            rows[p, h * BLK : (h + 1) * BLK, 0:DIM] = src[0:BLK, lanes]
            rows[p, h * BLK : (h + 1) * BLK, DIM : 2 * DIM] = src[BLK : 2 * BLK, lanes]
        cols[p] = rows[p].T

    spread(0, q_ref, qn, qt)
    local.wait()
    pltpu.make_async_remote_copy(
        src_ref=own,
        dst_ref=buf.at[3 - 3 * xx, 0],
        send_sem=ssem.at[0],
        recv_sem=rsem.at[0],
        device_id=xp,
        device_id_type=MESH,
    ).wait_recv()
    go("azp0", "azm0", "ay1", "ay2", "bz1", "bz2", "byp0", "bym0")

    got("q")
    spread(1, pq, qn, qt)
    got("ay1", "ay2", "bz1", "bz2")
    go("ay3", "azp1", "azm1", "azp2", "azm2", "bz3", "bz4", "byp1", "bym1", "byp2", "bym2")

    tok_k = lax.broadcasted_iota(jnp.int32, (BLK, ROWS), 0)
    tok_q = lax.broadcasted_iota(jnp.int32, (BLK, ROWS), 1) % BLK
    diag = tok_k <= tok_q
    for lh in range(2):
        s = jnp.where(diag, nt(own[lh], qt[0, lh * DIM : (lh + 1) * DIM]), NEG)
        m = row_max(s)
        p = jnp.exp2((s - m) * C2)
        stat[lh : lh + 1] = m
        stat[4 + lh : 5 + lh] = row_sum(p)
        ot[0, lh * DIM : (lh + 1) * DIM] = tn(own[2 + lh], p.astype(jnp.bfloat16))
    stat[2:4] = jnp.full((2, ROWS), NEG, jnp.float32)
    stat[6:8] = jnp.zeros((2, ROWS), jnp.float32)
    stat[12:16] = jnp.zeros((4, ROWS), jnp.float32)
    ot[1] = jnp.zeros((2 * DIM, ROWS), jnp.float32)

    got("ay3", "bz3", "bz4")
    go("azp3", "azm3", "bz5", "bz6", "byp3", "bym3")
    for c in (6, 9, 13, 14, 15):
        r1[c] = jnp.zeros((4, 4, BLK, DIM), jnp.bfloat16)
    r1[11, 2:4] = jnp.zeros((2, 4, BLK, DIM), jnp.bfloat16)
    r1[12, 0:2] = jnp.zeros((2, 4, BLK, DIM), jnp.bfloat16)

    def take(c):
        return [buf[c, :, kind].reshape(4 * BLK, DIM) for kind in range(4)]

    def picks(c, p):
        number = [kt[4 * c + w] for w in range(4)]
        return [n < ql[p] for n in number], [n == ql[p] for n in number]

    def cat(low, high, chosen):
        zero = jnp.zeros((BLK, DIM), jnp.bfloat16)
        rows = []
        for w in range(4):
            a, b = low[w * BLK : (w + 1) * BLK], high[w * BLK : (w + 1) * BLK]
            rows.append(
                jnp.concatenate(
                    [lax.select(chosen[w], a, zero), lax.select(chosen[w], zero, b)], axis=1
                )
            )
        return jnp.concatenate(rows, axis=0)

    neg_row = jnp.full((1, ROWS), NEG, jnp.float32)
    big_row = jnp.full((1, ROWS), BIG, jnp.float32)

    def windows(x):
        return [x[w * BLK : (w + 1) * BLK] for w in range(4)]

    def arrive(c):
        def do(at_chunk, *steps):
            @pl.when(c == at_chunk)
            def _():
                for step, names in steps:
                    step(*names)

        do(1, (got, ["azp%d" % w for w in range(4)]), (go, ["a7"]), (got, ["bz5", "bz6"]), (go, ["bz7"]))
        do(2, (got, ["azm%d" % w for w in range(4)]), (go, ["a8"]))
        do(4, (got, ["bz7"]), (go, ["b9", "b10"]))
        do(5, (got, ["byp%d" % w for w in range(4)]), (go, ["b13"]))
        do(6, (got, ["bym%d" % w for w in range(4)]))
        do(7, (got, ["a7"]), (go, ["a11"]))
        do(8, (got, ["a8"]), (go, ["a12"]))
        do(9, (got, ["b9"]))
        do(10, (got, ["b10"]), (go, ["b14"]))
        do(11, (got, ["a11"]), (go, ["a15p"]))
        do(12, (got, ["a12"]), (go, ["a15m"]))
        do(13, (got, ["b13"]))
        do(14, (got, ["b14"]))
        do(15, (got, ["a15p", "a15m"]))

    def forward(c, carry):
        arrive(c)
        kl, kh, vl, vh = take(c)
        for p in range(2):
            low, same = picks(c, p)
            kcat, vcat = cat(kl, kh, low), cat(vl, vh, low)
            s1 = nt(kl, qt[p, DIM : 2 * DIM])
            s2 = windows(nt(kcat, qt[p]))
            rl, rh = 2 * p, 2 * p + 1
            ml, mh = stat[rl : rl + 1], stat[rh : rh + 1]
            nl, nh = ml, jnp.maximum(mh, row_max(s1))
            for w in range(4):
                top = row_max(s2[w])
                nl = jnp.maximum(nl, lax.select(low[w], top, neg_row))
                nh = jnp.maximum(nh, lax.select(low[w] | same[w], neg_row, top))
            fl, fh = jnp.exp2((ml - nl) * C2), jnp.exp2((mh - nh) * C2)
            p1 = jnp.exp2((s1 - nh) * C2)
            tl, th = stat[4 + rl : 5 + rl] * fl, stat[4 + rh : 5 + rh] * fh + row_sum(p1)
            parts = []
            for w in range(4):
                ref = lax.select(same[w], big_row, lax.select(low[w], nl, nh))
                part = jnp.exp2((s2[w] - ref) * C2)
                total = row_sum(part)
                zero = jnp.zeros_like(total)
                tl = tl + lax.select(low[w], total, zero)
                th = th + lax.select(low[w], zero, total)
                parts.append(part.astype(jnp.bfloat16))
            stat[rl : rl + 1], stat[rh : rh + 1] = nl, nh
            stat[4 + rl : 5 + rl], stat[4 + rh : 5 + rh] = tl, th
            o1 = tn(vl, p1.astype(jnp.bfloat16))
            o2 = tn(vcat, jnp.concatenate(parts, axis=0))
            ot[p, 0:DIM] = ot[p, 0:DIM] * fl + o2[0:DIM]
            ot[p, DIM : 2 * DIM] = ot[p, DIM : 2 * DIM] * fh + (o1 + o2[DIM : 2 * DIM])
        return carry

    lax.fori_loop(0, CHUNKS, forward, 0)

    go("ot")
    spread(0, g_ref, gn, gt)
    got("g")
    spread(1, pg, gn, gt)
    for p in range(2):
        for lh in range(2):
            r = 2 * p + lh
            rows = slice(lh * DIM, (lh + 1) * DIM)
            stat[8 + r : 9 + r] = row_sum(ot[p, rows] * gt[p, rows].astype(jnp.float32))
    go("stat")
    got("stat")
    scale_mine, scale_other = [], []
    for p in range(2):
        for lh in range(2):
            r, other = 2 * p + lh, 2 * (1 - p) + lh
            ma, mb = stat[r : r + 1], pstat[other : other + 1]
            top = jnp.maximum(ma, mb)
            fa, fb = jnp.exp2((ma - top) * C2), jnp.exp2((mb - top) * C2)
            total = stat[4 + r : 5 + r] * fa + pstat[4 + other : 5 + other] * fb
            delta = stat[8 + r : 9 + r] * fa + pstat[8 + other : 9 + other] * fb
            lse[r : r + 1] = top + jnp.log(total) * (1.0 / SCALE)
            lse[4 + r : 5 + r] = delta / total
            if p == 0:
                scale_mine.append(fa / total)
                scale_other.append(fb / total)
    for lh in range(2):
        lse[8 + 2 * lh : 9 + 2 * lh] = scale_mine[lh]
        lse[9 + 2 * lh : 10 + 2 * lh] = scale_other[lh]

    dqt[1] = jnp.zeros((2 * DIM, ROWS), jnp.float32)
    for lh in range(2):
        rows = slice(lh * DIM, (lh + 1) * DIM)
        s = jnp.where(diag, nt(own[lh], qt[0, rows]), NEG)
        p = jnp.exp2((s - lse[lh : lh + 1]) * C2)
        ds = (p * (nt(own[2 + lh], gt[0, rows]) - lse[4 + lh : 5 + lh])).astype(jnp.bfloat16)
        dg[lh] = nt(ds, qn[0, :, rows])
        dg[2 + lh] = nt(p.astype(jnp.bfloat16), gn[0, :, rows])
        dqt[0, rows] = tn(own[lh], ds)

    def backward(step, carry):
        c = CHUNKS - 1 - step
        kl, kh, vl, vh = take(c)
        sums = None
        for p in range(2):
            low, same = picks(c, p)
            kcat, vcat = cat(kl, kh, low), cat(vl, vh, low)
            rl, rh = 2 * p, 2 * p + 1
            high = slice(DIM, 2 * DIM)
            p1 = jnp.exp2((nt(kl, qt[p, high]) - lse[rh : rh + 1]) * C2)
            ds1 = (p1 * (nt(vl, gt[p, high]) - lse[4 + rh : 5 + rh])).astype(jnp.bfloat16)
            s2 = windows(nt(kcat, qt[p]))
            g2 = windows(nt(vcat, gt[p]))
            ps, ds = [], []
            for w in range(4):
                ref = lax.select(
                    same[w], big_row, lax.select(low[w], lse[rl : rl + 1], lse[rh : rh + 1])
                )
                delta = lax.select(low[w], lse[4 + rl : 5 + rl], lse[4 + rh : 5 + rh])
                part = jnp.exp2((s2[w] - ref) * C2)
                ps.append(part.astype(jnp.bfloat16))
                ds.append((part * (g2[w] - delta)).astype(jnp.bfloat16))
            p2, ds2 = jnp.concatenate(ps, axis=0), jnp.concatenate(ds, axis=0)
            dqt[p, high] = dqt[p, high] + tn(kl, ds1)
            dqt[p] = dqt[p] + tn(kcat, ds2)
            ones = [nt(ds1, qn[p, :, high]), nt(p1.astype(jnp.bfloat16), gn[p, :, high])]
            twos = [nt(ds2, qn[p]), nt(p2, gn[p])]
            new = []
            for one, two in zip(ones, twos):
                zero = jnp.zeros((BLK, DIM), jnp.float32)
                lows, highs = [], []
                for w in range(4):
                    rows = slice(w * BLK, (w + 1) * BLK)
                    lows.append(one[rows] + lax.select(low[w], two[rows, 0:DIM], zero))
                    highs.append(lax.select(low[w], zero, two[rows, DIM : 2 * DIM]))
                new += [lows, highs]
            if sums is None:
                sums = new
            else:
                sums = [[a + b for a, b in zip(x, y)] for x, y in zip(sums, new)]
        for kind in range(4):
            for w in range(4):
                tf[c, w, kind] = sums[kind][w]

        def before(at_chunk, *names):
            @pl.when(c == at_chunk)
            def _():
                got(*names)

        before(11, "r15m")
        before(12, "r15p")
        before(7, "r11")
        before(8, "r12")
        before(1, "r7")
        before(2, "r8")
        before(5, "r13")
        before(10, "r14")

        @pl.when((c != 0) & (c != 3) & (c != 4))
        def _():
            snd[c] = (tf[c] + r1[c].astype(jnp.float32)).astype(jnp.bfloat16)

        def after(at_chunk, *names):
            @pl.when(c == at_chunk)
            def _():
                go(*names)

        after(15, "r15m", "r15p")
        for at_chunk in (11, 12, 7, 8, 1, 2, 13, 14, 5, 9, 6, 10):
            after(at_chunk, "r%d" % at_chunk)

        @pl.when(c == 2)
        def _():
            got("r9", "r10", "r5", "r6")
            chain(4, None, 0)
            chain(3, None, 4)

        @pl.when(c == 1)
        def _():
            chain(-3, 0, 1)
            chain(2, 4, 5)

        return carry

    def b_total(dz, *arrived):
        for c in (3, 4):
            for w in range(4):
                if TABLE[c][w][2] == dz:
                    total = tf[c, w] + r1[c, w].astype(jnp.float32)
                    total = total + r2[c - 2, w].astype(jnp.float32)
        for n in arrived:
            got("rz%d" % n)
            total = total + rz[n].astype(jnp.float32)
        return total

    def chain(dz, arrived, leaving):
        total = b_total(dz) if arrived is None else b_total(dz, arrived)
        sz[leaving] = total.astype(jnp.bfloat16)
        go("rz%d" % leaving)

    def a_total(w, *arrived):
        total = tf[0, w] + r1[0, w].astype(jnp.float32) + r2[0, w].astype(jnp.float32)
        for n in arrived:
            got("ry%d" % n)
            total = total + ry[n].astype(jnp.float32)
        return total

    def a_send(w, leaving, *arrived):
        sy[leaving] = a_total(w, *arrived).astype(jnp.bfloat16)
        go("ry%d" % leaving)

    lax.fori_loop(0, CHUNKS, backward, 0)

    go("dq")
    chain(-2, 1, 2)
    chain(1, 5, 6)
    got("r1", "r2")
    a_send(3, 0)
    a_send(2, 2)

    def store(ref, rows):
        for h in range(HEADS):
            lanes = slice(h * DIM, (h + 1) * DIM)
            ref[0:BLK, lanes] = rows[h * BLK : (h + 1) * BLK, 0:DIM]
            ref[BLK : 2 * BLK, lanes] = rows[h * BLK : (h + 1) * BLK, DIM : 2 * DIM]

    got("ot")
    halves = []
    for lh in range(2):
        rows = slice(lh * DIM, (lh + 1) * DIM)
        halves.append(
            ot[0, rows] * lse[8 + 2 * lh : 9 + 2 * lh] + pot[rows] * lse[9 + 2 * lh : 10 + 2 * lh]
        )
    store(att_ref, jnp.concatenate(halves, axis=0).T.astype(jnp.bfloat16))

    chain(-1, 2, 3)
    a_send(1, 1, 0)
    got("dq")
    store(dq_ref, ((dqt[0] + pdq[...]) * SCALE).T.astype(jnp.bfloat16))

    total_b = b_total(0, 3, 6)
    total_a = a_total(0, 1, 2)
    first = xx == 0
    xs[...] = lax.select(first, total_b, total_a).astype(jnp.bfloat16)
    go("rx")
    mine = lax.select(first, total_a, total_b) + dg[...]
    got("rx")
    mine = mine + rx[...].astype(jnp.float32)
    for lh in range(2):
        rows = slice(lh * BLK, (lh + 1) * BLK)
        dk_ref[rows, :] = (mine[lh] * SCALE).astype(jnp.bfloat16)
        dv_ref[rows, :] = mine[2 + lh].astype(jnp.bfloat16)
    for copy in msgs.values():
        copy.wait_send()


def body(queries, keys, values, grad_out, block_pos):
    vmem = pl.BlockSpec(memory_space=pltpu.VMEM)
    bf, f32 = jnp.bfloat16, jnp.float32
    window = (4, BLK, DIM)
    count = 80
    outs = pl.pallas_call(
        kernel,
        out_shape=[
            jax.ShapeDtypeStruct((2 * BLK, HEADS * DIM), bf),
            jax.ShapeDtypeStruct((2 * BLK, HEADS * DIM), bf),
            jax.ShapeDtypeStruct((2 * BLK, DIM), bf),
            jax.ShapeDtypeStruct((2 * BLK, DIM), bf),
        ],
        in_specs=[pl.BlockSpec(memory_space=pltpu.SMEM)] + [vmem] * 4,
        out_specs=[vmem] * 4,
        scratch_shapes=[
            pltpu.VMEM((CHUNKS, 4) + window, bf),
            pltpu.VMEM(window, bf),
            pltpu.VMEM((2 * BLK, HEADS * DIM), bf),
            pltpu.VMEM((2 * BLK, HEADS * DIM), bf),
            pltpu.VMEM((2, ROWS, 2 * DIM), bf),
            pltpu.VMEM((2, ROWS, 2 * DIM), bf),
            pltpu.VMEM((2, 2 * DIM, ROWS), bf),
            pltpu.VMEM((2, 2 * DIM, ROWS), bf),
            pltpu.VMEM((2, 2 * DIM, ROWS), f32),
            pltpu.VMEM((2, 2 * DIM, ROWS), f32),
            pltpu.VMEM((16, ROWS), f32),
            pltpu.VMEM((16, ROWS), f32),
            pltpu.VMEM((16, ROWS), f32),
            pltpu.VMEM((2 * DIM, ROWS), f32),
            pltpu.VMEM((2 * DIM, ROWS), f32),
            pltpu.VMEM((CHUNKS, 4) + window, f32),
            pltpu.VMEM((CHUNKS, 4) + window, bf),
            pltpu.VMEM((CHUNKS, 4) + window, bf),
            pltpu.VMEM((3, 4) + window, bf),
            pltpu.VMEM((3,) + window, bf),
            pltpu.VMEM((3,) + window, bf),
            pltpu.VMEM((7,) + window, bf),
            pltpu.VMEM((7,) + window, bf),
            pltpu.VMEM(window, bf),
            pltpu.VMEM(window, bf),
            pltpu.VMEM(window, f32),
            pltpu.SMEM((4 * CHUNKS,), jnp.int32),
            pltpu.SemaphoreType.DMA,
            pltpu.SemaphoreType.DMA((count,)),
            pltpu.SemaphoreType.DMA((count,)),
        ],
        compiler_params=pltpu.CompilerParams(
            collective_id=0, has_side_effects=True, vmem_limit_bytes=52 * 1024 * 1024
        ),
        name="attention",
    )(block_pos, queries[0], keys[0], values[0], grad_out[0])
    return tuple(out[None] for out in outs)


def solution(mesh):
    spec = P("inner", "outer", None)
    return jax.shard_map(
        body,
        mesh=mesh,
        in_specs=(spec, spec, spec, spec, P()),
        out_specs=(spec, spec, spec, spec),
        check_vma=False,
    )
```

time: 1190 us -> 111 us (0.09)
  waiting for transfers between devices: 558 us -> 0 us
  local copies, waits for them, and re-layouts: 280 us -> 6.72 us
  matrix products: 234 us -> 0 us
  Pallas kernels: 0 us -> 103 us
  other arithmetic: 90.1 us -> 0 us
  between operations: 16.9 us -> 0.65 us
    reduce_scatter x1 -> x0, waiting for transfers between devices: 348 us -> none  [body(): lax.psum_scatter(grads_storage, 'outer', scatter_dimension=0, tiled=True)]
    dot_general x231 -> x0, matrix products: 234 us -> none  [the longest x99 124 us: dot_rows(): lax.dot_general(left, right, (((1,), (1,)), ((), ())), preferred_element_...]
    all_gather x1 -> x0, waiting for transfers between devices: 208 us -> none  [body(): lax.all_gather(jnp.concatenate([lower_kv, upper_kv], axis=0), 'outer', ax...]
    gather x2 -> x0, local copies, waits for them, and re-layouts: 156 us -> none  [the longest x1 90.5 us: body(): sorted_places = key_places[key_order]]
    pallas_call x0 -> x1, Pallas kernels: none -> 103 us  [body(): pl.pallas_call(kernel, out_shape=[jax.ShapeDtypeStruct((2 * BLK, HEADS *...]
    scatter x1 -> x0, local copies, waits for them, and re-layouts: 74.8 us -> none  [body(): grads_storage = jnp.zeros_like(grads_sorted).at[key_order].set(grads_sorted)]
    dynamic_update_slice x33 -> x0, other arithmetic: 63.5 us -> none  [advance(): lax.dynamic_update_slice_in_dim(grads_now, previous + jnp.concatenate([ke...]
    while x34 -> x0, local copies, waits for them, and re-layouts: 17.6 us -> none  [the longest x1 17.5 us: attend_backward(): return lax.fori_loop(0, blocks, advance, initial)]
  transfers between devices with their start and end apart: 4 -> 0, of which waited for: 4 -> 0; matrix products, arithmetic and copies ran while one was open for 9% -> 0% of each run, Pallas kernels for 0% -> 0%
where the time goes in v1:
time: 111 us; the launch traced here: 110 us
  Pallas kernels  103 us (93%)
  local copies, waits for them, and re-layouts  6.72 us (6%)
    pallas_call x1, Pallas kernels, body(): pl.pallas_call(kernel, out_shape=[jax.ShapeDtypeStruct((2 * BLK, HEADS *...  103 us
    unnamed x14, local copies, waits for them, and re-layouts  6.72 us

profile of v1, /device:TPU:4, one launch (start us, length us, event | category | flops | bytes accessed | tf_op | source)
XLA Modules:
  0.0 110.1 jit_solution(4809331552505271942)
XLA Ops:
  0.6 0.0 copy-start.4
  0.6 0.7 copy-done.4
  1.3 0.0 copy-start
  1.3 0.9 copy-done
  2.3 0.0 copy-start.1
  2.3 0.9 copy-done.1
  3.2 0.0 copy-start.2
  3.2 0.8 copy-done.2
  4.0 0.0 copy-start.3
  4.0 0.8 copy-done.3
  4.7 102.7 %attention.1 = (bf16[128,1024]{1,0:T(8,128)(2,1)S(1)}, bf16[128,1024]{1,0:T(8,128)(2,1)S(1)}, bf16[128,128]{1,0:T(8,128)(2,1)S(1)}, bf16[128,128]{1,0:T(8,128)(2,1)S(1)}) custom-call(s32[4,128]{1,0:T(4,128)S(1)} %copy-done.4, bf16[128,1024]{1,0:T(8,128)(2,1)S(1)} %bitcast.8, bf16[128,128]{1,0:T(8,128)(2,1)S(1)} %bitcast.12, bf16[128,128]{1,0:T(8,128)(2,1)S(1)} %bitcast.13, ...), custom_call_target="tpu_custom_call" | custom-call | tf_op jit(solution)/shard_map/attention/pallas_call | solution.py:545
  107.4 0.7 copy.13
  108.1 0.7 copy.14
  108.8 0.6 copy.15
  109.4 0.6 copy.16
Async XLA Ops:
  0.6 0.7 copy-start.4
  1.3 0.9 copy-start
  2.3 0.9 copy-start.1
  3.2 0.8 copy-start.2
  4.0 0.8 copy-start.3

commit v2 on v1

v2 whole, which is shorter than its diff:
```python
import jax
import jax.numpy as jnp
from jax import lax
from jax.experimental import pallas as pl
from jax.experimental.pallas import tpu as pltpu
from jax.sharding import PartitionSpec as P

MESH = pl.DeviceIdType.MESH
NEG = -1e30
BIG = 1e30
BLK = 64
HALF = 32
DIM = 128
HEADS = 8
ROWS = BLK * HEADS
CHUNKS = 16
STEPS = 8
KEYS = 8 * HALF
SCALE = DIM**-0.5
C2 = SCALE * 1.4426950408889634

YORDER = (0, -1, 1, 2)
NEAR = (0, -1, 1, -2)
FAR = (2, -3, 3, 4)


def a_chunk(dz):
    return [(dy, dz) for dy in YORDER]


def b_chunk(dy, part):
    return [(dy, dz) for dz in part]


TABLE = [
    a_chunk(0),
    b_chunk(0, NEAR),
    a_chunk(-1),
    a_chunk(1),
    b_chunk(0, FAR),
    b_chunk(-1, NEAR),
    b_chunk(1, NEAR),
    a_chunk(-2),
    a_chunk(2),
    b_chunk(-1, FAR),
    b_chunk(1, FAR),
    a_chunk(-3),
    a_chunk(3),
    b_chunk(2, NEAR),
    b_chunk(2, FAR),
    a_chunk(4),
]


def nt(a, b):
    return lax.dot_general(a, b, (((1,), (0,)), ((), ())), preferred_element_type=jnp.float32)


def tn(a, b):
    return lax.dot_general(a, b, (((0,), (0,)), ((), ())), preferred_element_type=jnp.float32)


def fold(x, op):
    rows, lanes = x.shape
    return op(x.reshape(rows // 8, 8, lanes), axis=0)


def row_sum(x):
    return jnp.sum(x, axis=0, keepdims=True)


def row_max(x):
    return jnp.max(x, axis=0, keepdims=True)


def kernel(
    pos_ref,
    q_ref,
    k_ref,
    v_ref,
    g_ref,
    att_ref,
    dq_ref,
    dk_ref,
    dv_ref,
    buf,
    mq,
    mg,
    pq,
    pg,
    qn,
    gn,
    qt,
    gt,
    ot,
    dqt,
    stat,
    ls,
    pstat,
    lse,
    mc,
    wt,
    pot,
    pd,
    xd,
    px,
    tf,
    snd,
    r1,
    r2,
    sy,
    ry,
    sz,
    rz,
    dg,
    pos,
    kt,
    lsem,
    ssem,
    rsem,
):
    outer = lax.axis_index("outer")
    inner = lax.axis_index("inner")
    yy = outer // 16
    xx = (outer // 8) % 2
    zz = outer % 8
    mate = inner + 1 - 2 * (inner % 2)

    def at(x, dy, dz):
        return (((yy + dy + 4) % 4) * 2 + x) * 8 + (zz + dz + 8) % 8

    beside = at(1 - xx, 0, 0)
    yp, ym = (at(xx, 1, 0), inner), (at(xx, -1, 0), inner)
    zp, zm = (at(xx, 0, 1), inner), (at(xx, 0, -1), inner)
    cp, xp, dp = (outer, mate), (beside, inner), (beside, mate)

    barrier = pltpu.get_barrier_semaphore()
    for dev in (yp, ym, zp, zm, cp, xp, dp):
        pl.semaphore_signal(barrier, inc=1, device_id=dev, device_id_type=MESH)

    fetch = [
        pltpu.make_async_copy(pos_ref, pos, lsem.at[0]),
        pltpu.make_async_copy(q_ref, mq, lsem.at[1]),
        pltpu.make_async_copy(g_ref, mg, lsem.at[2]),
    ]
    pieces = []
    for n, ref in enumerate((k_ref, v_ref)):
        for lh in range(2):
            for half in range(2):
                pieces.append(
                    pltpu.make_async_copy(
                        ref.at[pl.ds(lh * BLK + half * HALF, HALF)],
                        buf.at[half, 0, 2 * n + lh],
                        lsem.at[3 + len(pieces)],
                    )
                )
    for copy in pieces + fetch:
        copy.start()
    pl.semaphore_wait(barrier, 7)

    msgs = {}

    def msg(name, src, dst, dev):
        at_sem = len(msgs)
        msgs[name] = pltpu.make_async_remote_copy(
            src_ref=src,
            dst_ref=dst,
            send_sem=ssem.at[at_sem],
            recv_sem=rsem.at[at_sem],
            device_id=dev,
            device_id_type=MESH,
        )

    def go(*names):
        for name in names:
            msgs[name].start()

    def got(*names):
        for name in names:
            msgs[name].wait_recv()

    for name, src, dst in (("q", q_ref, pq), ("g", g_ref, pg)):
        msg(name + "1", src, dst.at[0], cp)
        msg(name + "2", src, dst.at[1], xp)
        msg(name + "3", dst.at[1], dst.at[2], cp)
    msg("ay1", buf.at[0, 0], buf.at[0, 1], yp)
    msg("ay2", buf.at[0, 0], buf.at[0, 2], ym)
    msg("ay3", buf.at[0, 1], buf.at[0, 3], yp)
    for w in range(4):
        msg("azp%d" % w, buf.at[0, w], buf.at[2, w], zp)
        msg("azm%d" % w, buf.at[0, w], buf.at[3, w], zm)
        msg("byp%d" % w, buf.at[1, w], buf.at[5, w], yp)
        msg("bym%d" % w, buf.at[1, w], buf.at[6, w], ym)
    msg("a7", buf.at[2], buf.at[7], zp)
    msg("a8", buf.at[3], buf.at[8], zm)
    msg("a11", buf.at[7], buf.at[11], zp)
    msg("a12", buf.at[8], buf.at[12], zm)
    msg("a15p", buf.at[11, pl.ds(0, 2)], buf.at[15, pl.ds(0, 2)], zp)
    msg("a15m", buf.at[12, pl.ds(2, 2)], buf.at[15, pl.ds(2, 2)], zm)
    msg("bz1", buf.at[1, 0], buf.at[1, 1], zp)
    msg("bz2", buf.at[1, 0], buf.at[1, 2], zm)
    msg("bz3", buf.at[1, 1], buf.at[1, 3], zp)
    msg("bz4", buf.at[1, 2], buf.at[4, 0], zm)
    msg("bz5", buf.at[1, 3], buf.at[4, 1], zp)
    msg("bz6", buf.at[4, 0], buf.at[4, 2], zm)
    msg("bz7", buf.at[4, 1], buf.at[4, 3], zp)
    msg("b9", buf.at[4], buf.at[9], yp)
    msg("b10", buf.at[4], buf.at[10], ym)
    msg("b13", buf.at[5], buf.at[13], yp)
    msg("b14", buf.at[10], buf.at[14], ym)
    for n, dev in enumerate((cp, xp, dp)):
        msg("stat%d" % n, stat, pstat.at[n], dev)
    for n, dev in enumerate((cp, xp, dp)):
        msg("ot%d" % n, ot.at[n + 1], pot.at[n], dev)
    msg("dq3", dqt.at[3], pd.at[0], cp)
    msg("dq2", xd, px, xp)
    msg("dq1", dqt.at[1], pd.at[1], cp)
    msg("r15m", snd.at[15, pl.ds(0, 2)], r1.at[11, pl.ds(0, 2)], zm)
    msg("r15p", snd.at[15, pl.ds(2, 2)], r1.at[12, pl.ds(2, 2)], zp)
    msg("r11", snd.at[11], r1.at[7], zm)
    msg("r12", snd.at[12], r1.at[8], zp)
    msg("r7", snd.at[7], r1.at[2], zm)
    msg("r8", snd.at[8], r1.at[3], zp)
    msg("r2", snd.at[2], r1.at[0], zm)
    msg("r3", snd.at[3], r2.at[0], zp)
    msg("r13", snd.at[13], r1.at[5], ym)
    msg("r14", snd.at[14], r1.at[10], yp)
    msg("r5", snd.at[5], r1.at[1], ym)
    msg("r9", snd.at[9], r1.at[4], ym)
    msg("r6", snd.at[6], r2.at[1], yp)
    msg("r10", snd.at[10], r2.at[2], yp)
    for n, dev in enumerate((ym, ym, yp)):
        msg("ry%d" % n, sy.at[n], ry.at[n], dev)
    for n, dev in enumerate((zm, zm, zm, zm, zp, zp, zp)):
        msg("rz%d" % n, sz.at[n], rz.at[n], dev)

    go("q2", "q1")
    for copy in pieces:
        copy.wait()
    go("ay1", "ay2", "bz1", "bz2", "azp0", "azm0", "byp0", "bym0", "g2", "g1")
    fetch[0].wait()

    for p, (row, column) in enumerate(
        ((inner, outer), (mate, outer), (inner, beside), (mate, beside))
    ):
        kt[4 * CHUNKS + p] = pos[row, 2 * column]
    for c in range(CHUNKS):
        for w in range(4):
            dy, dz = TABLE[c][w]
            kt[4 * c + w] = pos[inner, 2 * at(xx, dy, dz)]

    def spread(p, src, rows, cols):
        for h in range(HEADS):
            lanes = slice(h * DIM, (h + 1) * DIM)
            rows[p, h * BLK : (h + 1) * BLK, 0:DIM] = src[0:BLK, lanes]
            rows[p, h * BLK : (h + 1) * BLK, DIM : 2 * DIM] = src[BLK : 2 * BLK, lanes]
        cols[p] = rows[p].T

    fetch[1].wait()
    spread(0, mq, qn, qt)
    got("ay1", "ay2", "bz1", "bz2")
    go("ay3", "bz3", "bz4", "azp1", "azm1", "azp2", "azm2", "byp1", "bym1", "byp2", "bym2")
    got("q1")
    spread(1, pq.at[0], qn, qt)

    tok_k = lax.broadcasted_iota(jnp.int32, (BLK, ROWS), 0)
    tok_q = lax.broadcasted_iota(jnp.int32, (BLK, ROWS), 1) % BLK
    diag = tok_k <= tok_q

    def own(kind):
        return jnp.concatenate([buf[0, 0, kind], buf[1, 0, kind]], axis=0)

    for lh in range(2):
        s = jnp.where(diag, nt(own(lh), qt[0, lh * DIM : (lh + 1) * DIM]), NEG)
        m = row_max(s)
        p = jnp.exp2((s - m) * C2)
        stat[lh : lh + 1] = m
        ls[lh] = fold(p, jnp.sum)
        ot[0, lh * DIM : (lh + 1) * DIM] = tn(own(2 + lh), p.astype(jnp.bfloat16))
    stat[2:8] = jnp.full((6, ROWS), NEG, jnp.float32)
    ls[2:8] = jnp.zeros((6, 8, ROWS), jnp.float32)

    fetch[2].wait()
    spread(0, mg, gn, gt)
    got("ay3", "bz3", "bz4")
    go("azp3", "azm3", "bz5", "bz6", "byp3", "bym3")
    for p in range(1, 4):
        ot[p] = jnp.zeros((2 * DIM, ROWS), jnp.float32)
    for c in (6, 9, 13, 14, 15):
        r1[c] = jnp.zeros((4, 4, HALF, DIM), jnp.bfloat16)
    r1[11, 2:4] = jnp.zeros((2, 4, HALF, DIM), jnp.bfloat16)
    r1[12, 0:2] = jnp.zeros((2, 4, HALF, DIM), jnp.bfloat16)

    def take(i, kind):
        return buf[pl.ds(2 * i, 2), :, kind].reshape(KEYS, DIM)

    def picks(i, p):
        number = [kt[8 * i + w] for w in range(8)]
        mine = kt[4 * CHUNKS + p]
        return [n < mine for n in number], [n == mine for n in number]

    def windows(x):
        return [x[w * HALF : (w + 1) * HALF] for w in range(8)]

    def cat(low, high, chosen):
        zero = jnp.zeros((HALF, DIM), jnp.bfloat16)
        rows = []
        for a, b, pick in zip(windows(low), windows(high), chosen):
            rows.append(
                jnp.concatenate([lax.select(pick, a, zero), lax.select(pick, zero, b)], axis=1)
            )
        return jnp.concatenate(rows, axis=0)

    neg_rows = jnp.full((8, ROWS // 2), NEG, jnp.float32)
    big_row = jnp.full((1, ROWS // 2), BIG, jnp.float32)
    high = slice(DIM, 2 * DIM)

    def row(ref, r):
        return ref[pl.ds(r, 1)]

    def arrive(n):
        def do(at_step, *steps):
            @pl.when(n == at_step)
            def _():
                for step, names in steps:
                    step(*names)

        quads = range(4)

        @pl.when(n == 1)
        def _():
            got("q2")
            go("q3")
            spread(2, pq.at[1], qn, qt)
            got("q3")
            spread(3, pq.at[2], qn, qt)

        do(2, (got, ["azp%d" % w for w in quads] + ["azm%d" % w for w in quads]), (go, ["a7", "a8"]))
        do(2, (got, ["bz5", "bz6"]), (go, ["bz7"]))
        do(4, (got, ["bz7"]), (go, ["b9", "b10"]), (got, ["byp%d" % w for w in quads]), (go, ["b13"]))
        do(5, (got, ["g2"]), (go, ["g3"]))

        @pl.when(n == 9)
        def _():
            got("g1", "g3")
            for p in range(1, 4):
                spread(p, pg.at[p - 1], gn, gt)

        do(6, (got, ["bym%d" % w for w in quads] + ["a7", "a8"]), (go, ["a11", "a12"]))
        do(8, (got, ["b9"]))
        do(9, (got, ["b10"]), (go, ["b14"]))
        do(10, (got, ["a11", "a12"]), (go, ["a15p", "a15m"]))
        do(12, (got, ["b13"]))
        do(14, (got, ["b14", "a15p", "a15m"]))

    def forward(n, carry):
        arrive(n)
        i = n // 2
        kl, kh, vl, vh = [take(i, kind) for kind in range(4)]
        parts = []
        for unrolled in range(2):
            p = 2 * (n % 2) + unrolled
            low, same = picks(i, p)
            kcat, vcat = cat(kl, kh, low), cat(vl, vh, low)
            for lanes in (slice(0, ROWS // 2), slice(ROWS // 2, ROWS)):
                olds = [stat[pl.ds(2 * p + lh, 1), lanes] for lh in range(2)]
                parts.append((p, lanes, low, same, kcat, vcat, olds))

        def scores(part):
            p, lanes, _, _, kcat, _, _ = part
            return nt(kl, qt[p, high, lanes]), windows(nt(kcat, qt[p, :, lanes]))

        def weigh(part, s1, s2):
            p, lanes, low, same, _, vcat, (ml, mh) = part
            rl, rh = 2 * p, 2 * p + 1
            tops_l, tops_h = neg_rows, fold(s1, jnp.max)
            for w in range(8):
                top = fold(s2[w], jnp.max)
                tops_l = jnp.maximum(tops_l, lax.select(low[w], top, neg_rows))
                tops_h = jnp.maximum(tops_h, lax.select(low[w] | same[w], neg_rows, top))
            nl, nh = jnp.maximum(ml, row_max(tops_l)), jnp.maximum(mh, row_max(tops_h))
            fl, fh = jnp.exp2((ml - nl) * C2), jnp.exp2((mh - nh) * C2)
            p1 = jnp.exp2((s1 - nh) * C2)
            tl, th = ls[rl, :, lanes] * fl, ls[rh, :, lanes] * fh + fold(p1, jnp.sum)
            pieces = []
            for w in range(8):
                ref = lax.select(same[w], big_row, lax.select(low[w], nl, nh))
                piece = jnp.exp2((s2[w] - ref) * C2)
                total = fold(piece, jnp.sum)
                zero = jnp.zeros_like(total)
                tl = tl + lax.select(low[w], total, zero)
                th = th + lax.select(low[w], zero, total)
                pieces.append(piece.astype(jnp.bfloat16))
            ls[rl, :, lanes], ls[rh, :, lanes] = tl, th
            stat[pl.ds(rl, 1), lanes], stat[pl.ds(rh, 1), lanes] = nl, nh
            mc[i, pl.ds(rl, 1), lanes], mc[i, pl.ds(rh, 1), lanes] = nl, nh
            w1, w2 = p1.astype(jnp.bfloat16), jnp.concatenate(pieces, axis=0)
            wt[i, p, 0, :, lanes], wt[i, p, 1, :, lanes] = w1, w2
            return p, lanes, fl, fh, tn(vl, w1), tn(vcat, w2)

        def update(p, lanes, fl, fh, o1, o2):
            ot[p, 0:DIM, lanes] = ot[p, 0:DIM, lanes] * fl + o2[0:DIM]
            ot[p, high, lanes] = ot[p, high, lanes] * fh + (o1 + o2[high])

        now, late = scores(parts[0]), None
        for k in range(4):
            later = scores(parts[k + 1]) if k < 3 else None
            done = weigh(parts[k], *now)
            if late is not None:
                update(*late)
            now, late = later, done
        update(*late)
        return carry

    lax.fori_loop(0, 2 * STEPS, forward, 0)

    for p in range(4):
        for lh in range(2):
            r = 2 * p + lh
            stat[8 + r : 9 + r] = row_sum(ls[r])
            rows = slice(lh * DIM, (lh + 1) * DIM)
            stat[16 + r : 17 + r] = row_sum(ot[p, rows] * gt[p, rows].astype(jnp.float32))
    go("stat2", "stat1", "stat0")
    go("ot0", "ot1", "ot2")

    dqt[1:4] = jnp.zeros((3, 2 * DIM, ROWS), jnp.float32)
    got("stat0", "stat1", "stat2")
    for p in range(4):
        for lh in range(2):
            r = 2 * p + lh
            held = [(stat, r)] + [(pstat.at[n - 1], 2 * (p ^ n) + lh) for n in range(1, 4)]
            tops = [row(ref, at_row) for ref, at_row in held]
            top = jnp.maximum(jnp.maximum(tops[0], tops[1]), jnp.maximum(tops[2], tops[3]))
            factors = [jnp.exp2((m - top) * C2) for m in tops]
            total, delta = 0.0, 0.0
            for factor, (ref, at_row) in zip(factors, held):
                total = total + factor * row(ref, 8 + at_row)
                delta = delta + factor * row(ref, 16 + at_row)
            lse[r : r + 1] = top + jnp.log(total) * (1.0 / SCALE)
            lse[8 + r : 9 + r] = delta / total
            if p == 0:
                for n in range(4):
                    lse[16 + 2 * n + lh : 17 + 2 * n + lh] = factors[n] / total

    for lh in range(2):
        rows = slice(lh * DIM, (lh + 1) * DIM)
        s = jnp.where(diag, nt(own(lh), qt[0, rows]), NEG)
        p = jnp.exp2((s - lse[lh : lh + 1]) * C2)
        ds = (p * (nt(own(2 + lh), gt[0, rows]) - lse[8 + lh : 9 + lh])).astype(jnp.bfloat16)
        dk = nt(ds, qn[0, :, rows])
        dv = nt(p.astype(jnp.bfloat16), gn[0, :, rows])
        for half in range(2):
            dg[half, lh] = dk[half * HALF : (half + 1) * HALF]
            dg[half, 2 + lh] = dv[half * HALF : (half + 1) * HALF]
        dqt[0, rows] = tn(own(lh), ds)

    def total_of(c, w, slot, ref, *arrived):
        total = tf[c, w] + r1[c, w].astype(jnp.float32) + r2[slot, w].astype(jnp.float32)
        for n in arrived:
            total = total + ref[n].astype(jnp.float32)
        return total

    def b_total(dz, *arrived):
        got(*["rz%d" % n for n in arrived])
        for slot, c in ((1, 1), (2, 4)):
            for w in range(4):
                if TABLE[c][w][1] == dz:
                    return total_of(c, w, slot, rz, *arrived)

    def chain(dz, leaving, *arrived):
        sz[leaving] = b_total(dz, *arrived).astype(jnp.bfloat16)
        go("rz%d" % leaving)

    def a_total(w, *arrived):
        got(*["ry%d" % n for n in arrived])
        return total_of(0, w, 0, ry, *arrived)

    def a_send(w, leaving, *arrived):
        sy[leaving] = a_total(w, *arrived).astype(jnp.bfloat16)
        go("ry%d" % leaving)

    def backward(n, carry):
        i = STEPS - 1 - n // 2
        vl, vh = take(i, 2), take(i, 3)
        parts = []
        for unrolled in range(2):
            p = 2 * (n % 2) + unrolled
            low, same = picks(i, p)
            vcat = cat(vl, vh, low)
            for lanes in (slice(0, ROWS // 2), slice(ROWS // 2, ROWS)):
                parts.append((p, lanes, low, vcat))

        def dots(part):
            p, lanes, _, vcat = part
            return nt(vl, gt[p, high, lanes]), windows(nt(vcat, gt[p, :, lanes]))

        def work(part, g1, g2):
            p, lanes, low, _ = part
            rl, rh = 2 * p, 2 * p + 1
            el, eh = lse[pl.ds(8 + rl, 1), lanes], lse[pl.ds(8 + rh, 1), lanes]
            fl = jnp.exp2((mc[i, pl.ds(rl, 1), lanes] - lse[pl.ds(rl, 1), lanes]) * C2)
            fh = jnp.exp2((mc[i, pl.ds(rh, 1), lanes] - lse[pl.ds(rh, 1), lanes]) * C2)
            p1 = wt[i, p, 0, :, lanes].astype(jnp.float32) * fh
            ds1 = (p1 * (g1 - eh)).astype(jnp.bfloat16)
            w2 = windows(wt[i, p, 1, :, lanes].astype(jnp.float32))
            ps, ds = [], []
            for w in range(8):
                piece = w2[w] * lax.select(low[w], fl, fh)
                ps.append(piece.astype(jnp.bfloat16))
                ds.append((piece * (g2[w] - lax.select(low[w], el, eh))).astype(jnp.bfloat16))
            p2, ds2 = jnp.concatenate(ps, axis=0), jnp.concatenate(ds, axis=0)
            wt[i, p, 0, :, lanes], wt[i, p, 1, :, lanes] = ds1, ds2
            return p1.astype(jnp.bfloat16), ds1, p2, ds2

        def products(p, low, left, right):
            p1, ds1, p2, ds2 = [jnp.concatenate([a, b], axis=1) for a, b in zip(left, right)]
            new = []
            for one, two in (
                (nt(ds1, qn[p, :, high]), nt(ds2, qn[p])),
                (nt(p1, gn[p, :, high]), nt(p2, gn[p])),
            ):
                zero = jnp.zeros((HALF, DIM), jnp.float32)
                lows, highs = [], []
                for w in range(8):
                    rows = slice(w * HALF, (w + 1) * HALF)
                    lows.append(one[rows] + lax.select(low[w], two[rows, 0:DIM], zero))
                    highs.append(lax.select(low[w], zero, two[rows, high]))
                new += [lows, highs]
            return new

        dot0, dot1 = dots(parts[0]), dots(parts[1])
        work0 = work(parts[0], *dot0)
        dot2 = dots(parts[2])
        work1 = work(parts[1], *dot1)
        dot3 = dots(parts[3])
        sums = products(parts[0][0], parts[0][2], work0, work1)
        work2 = work(parts[2], *dot2)
        work3 = work(parts[3], *dot3)
        others = products(parts[2][0], parts[2][2], work2, work3)
        sums = [[a + b for a, b in zip(x, y)] for x, y in zip(sums, others)]

        @pl.when(n % 2 == 0)
        def _():
            for kind in range(4):
                for w in range(8):
                    tf[2 * i + w // 4, w % 4, kind] = sums[kind][w]

        @pl.when(n % 2 == 1)
        def _():
            for kind in range(4):
                for w in range(8):
                    at_chunk = 2 * i + w // 4
                    tf[at_chunk, w % 4, kind] = tf[at_chunk, w % 4, kind] + sums[kind][w]

        def add(c):
            snd[c] = (tf[c] + r1[c].astype(jnp.float32)).astype(jnp.bfloat16)

        def finish(at_step, *chunks):
            @pl.when(n == 2 * (STEPS - 1 - at_step) + 1)
            def _():
                for c, waits, sends in chunks:
                    got(*waits)
                    add(c)
                    go(*sends)

        finish(7, (15, [], ["r15m", "r15p"]), (14, [], ["r14"]))
        finish(6, (13, [], ["r13"]), (12, ["r15p"], ["r12"]))
        finish(5, (11, ["r15m"], ["r11"]), (10, ["r14"], ["r10"]))
        finish(4, (9, [], ["r9"]), (8, ["r12"], ["r8"]))
        finish(3, (6, [], ["r6"]), (7, ["r11"], ["r7"]))
        finish(2, (5, ["r13"], ["r5"]))
        finish(1, (2, ["r7"], ["r2"]), (3, ["r8"], ["r3"]))

        @pl.when(n == 2 * (STEPS - 1 - 2) + 1)
        def _():
            got("r9", "r10")
            chain(4, 0)
            chain(3, 4)

        @pl.when(n == 2 * (STEPS - 1 - 1) + 1)
        def _():
            chain(-3, 1, 0)
            chain(2, 5, 4)

        return carry

    lax.fori_loop(0, 2 * STEPS, backward, 0)

    def store(ref, rows):
        for h in range(HEADS):
            lanes = slice(h * DIM, (h + 1) * DIM)
            ref[0:BLK, lanes] = rows[h * BLK : (h + 1) * BLK, 0:DIM]
            ref[BLK : 2 * BLK, lanes] = rows[h * BLK : (h + 1) * BLK, DIM : 2 * DIM]

    def attend():
        got("ot0", "ot1", "ot2")
        halves = []
        for lh in range(2):
            rows = slice(lh * DIM, (lh + 1) * DIM)
            total = ot[0, rows] * lse[16 + lh : 17 + lh]
            for n in range(1, 4):
                total = total + pot[n - 1, rows] * lse[16 + 2 * n + lh : 17 + 2 * n + lh]
            halves.append(total)
        store(att_ref, jnp.concatenate(halves, axis=0).T.astype(jnp.bfloat16))

    def queries_back(n, carry):
        def stage(at_step):
            return pl.when(n == at_step)

        @stage(0)
        def _():
            got("r5", "r6")
            chain(-2, 2, 1)
            chain(1, 6, 5)

        @stage(1)
        def _():
            attend()
            got("r2", "r3")
            a_send(3, 0)
            a_send(2, 2)

        @stage(2)
        def _():
            go("dq3")

        @stage(3)
        def _():
            a_send(1, 1, 0)
            chain(-1, 3, 2)

        @stage(4)
        def _():
            got("dq3")
            xd[...] = (dqt[2] + pd[0]).astype(jnp.bfloat16)
            go("dq2")

        @stage(6)
        def _():
            go("dq1")

        p = 3 - n // 2
        lows, cats, d1, d2 = [], [], [], []
        for k in range(4):
            i = 4 * (n % 2) + k
            kl, kh = take(i, 0), take(i, 1)
            low, same = picks(i, p)
            lows.append(kl)
            cats.append(cat(kl, kh, low))
            d1.append(wt[i, p, 0])
            d2.append(wt[i, p, 1])
        one = tn(jnp.concatenate(lows, axis=0), jnp.concatenate(d1, axis=0))
        two = tn(jnp.concatenate(cats, axis=0), jnp.concatenate(d2, axis=0))
        dqt[p, 0:DIM] = dqt[p, 0:DIM] + two[0:DIM]
        dqt[p, high] = dqt[p, high] + (one + two[high])
        return carry

    lax.fori_loop(0, 8, queries_back, 0)

    for half, total in enumerate((a_total(0, 1, 2), b_total(0, 3, 6))):
        total = total + dg[half]
        for lh in range(2):
            rows = slice(lh * BLK + half * HALF, lh * BLK + (half + 1) * HALF)
            dk_ref[rows, :] = (total[lh] * SCALE).astype(jnp.bfloat16)
            dv_ref[rows, :] = total[2 + lh].astype(jnp.bfloat16)

    got("dq2", "dq1")
    total = dqt[0] + pd[1] + px[...].astype(jnp.float32)
    store(dq_ref, (total * SCALE).T.astype(jnp.bfloat16))
    for copy in msgs.values():
        copy.wait_send()


def hand_out(*refs):
    sources, targets, sems = refs[:4], refs[4:8], refs[8]
    copies = [
        pltpu.make_async_copy(src, dst, sems.at[n])
        for n, (src, dst) in enumerate(zip(sources, targets))
    ]
    for copy in copies:
        copy.start()
    for copy in copies:
        copy.wait()


def body(queries, keys, values, grad_out, block_pos):
    vmem = pl.BlockSpec(memory_space=pltpu.VMEM)
    bf, f32 = jnp.bfloat16, jnp.float32
    window = (4, HALF, DIM)
    raw = (2 * BLK, HEADS * DIM)
    count = 80
    shapes = [
        jax.ShapeDtypeStruct(raw, bf),
        jax.ShapeDtypeStruct(raw, bf),
        jax.ShapeDtypeStruct((2 * BLK, DIM), bf),
        jax.ShapeDtypeStruct((2 * BLK, DIM), bf),
    ]
    outs = pl.pallas_call(
        kernel,
        out_shape=shapes,
        in_specs=[pl.BlockSpec(memory_space=pltpu.HBM)] * 5,
        out_specs=[vmem] * 4,
        scratch_shapes=[
            pltpu.VMEM((CHUNKS, 4) + window, bf),
            pltpu.VMEM(raw, bf),
            pltpu.VMEM(raw, bf),
            pltpu.VMEM((3,) + raw, bf),
            pltpu.VMEM((3,) + raw, bf),
            pltpu.VMEM((4, ROWS, 2 * DIM), bf),
            pltpu.VMEM((4, ROWS, 2 * DIM), bf),
            pltpu.VMEM((4, 2 * DIM, ROWS), bf),
            pltpu.VMEM((4, 2 * DIM, ROWS), bf),
            pltpu.VMEM((4, 2 * DIM, ROWS), f32),
            pltpu.VMEM((4, 2 * DIM, ROWS), f32),
            pltpu.VMEM((24, ROWS), f32),
            pltpu.VMEM((8, 8, ROWS), f32),
            pltpu.VMEM((3, 24, ROWS), f32),
            pltpu.VMEM((24, ROWS), f32),
            pltpu.VMEM((STEPS, 8, ROWS), f32),
            pltpu.VMEM((STEPS, 4, 2, KEYS, ROWS), bf),
            pltpu.VMEM((3, 2 * DIM, ROWS), f32),
            pltpu.VMEM((2, 2 * DIM, ROWS), f32),
            pltpu.VMEM((2 * DIM, ROWS), bf),
            pltpu.VMEM((2 * DIM, ROWS), bf),
            pltpu.VMEM((CHUNKS, 4) + window, f32),
            pltpu.VMEM((CHUNKS, 4) + window, bf),
            pltpu.VMEM((CHUNKS, 4) + window, bf),
            pltpu.VMEM((3, 4) + window, bf),
            pltpu.VMEM((3,) + window, bf),
            pltpu.VMEM((3,) + window, bf),
            pltpu.VMEM((7,) + window, bf),
            pltpu.VMEM((7,) + window, bf),
            pltpu.VMEM((2,) + window, f32),
            pltpu.SMEM((4, 2 * BLK), jnp.int32),
            pltpu.SMEM((4 * CHUNKS + 4,), jnp.int32),
            pltpu.SemaphoreType.DMA((11,)),
            pltpu.SemaphoreType.DMA((count,)),
            pltpu.SemaphoreType.DMA((count,)),
        ],
        compiler_params=pltpu.CompilerParams(
            collective_id=0, has_side_effects=True, vmem_limit_bytes=54 * 1024 * 1024
        ),
        name="attention",
    )(block_pos, queries[0], keys[0], values[0], grad_out[0])
    outs = pl.pallas_call(
        hand_out,
        out_shape=shapes,
        in_specs=[pl.BlockSpec(memory_space=pl.ANY)] * 4,
        out_specs=[pl.BlockSpec(memory_space=pltpu.HBM)] * 4,
        scratch_shapes=[pltpu.SemaphoreType.DMA((4,))],
        name="hand_out",
    )(*outs)
    return tuple(out[None] for out in outs)


def solution(mesh):
    spec = P("inner", "outer", None)
    return jax.shard_map(
        body,
        mesh=mesh,
        in_specs=(spec, spec, spec, spec, P()),
        out_specs=(spec, spec, spec, spec),
        check_vma=False,
    )
```

time: 111 us -> 103 us (0.928)
  local copies, waits for them, and re-layouts: 6.72 us -> 0 us
    unnamed x14 -> x0, local copies, waits for them, and re-layouts: 6.72 us -> none
    pallas_call x1 -> x2, Pallas kernels: 103 us -> 102 us  [the longest x1 82.8 us: body(): pl.pallas_call(kernel, out_shape=shapes, in_specs=[pl.BlockSpec(memory_sp...]
where the time goes in v2:
time: 103 us; the launch traced here: 102 us
  Pallas kernels  102 us (99%)
    pallas_call x1, Pallas kernels, body(): pl.pallas_call(kernel, out_shape=shapes, in_specs=[pl.BlockSpec(memory_sp...  82.8 us
    pallas_call x1, Pallas kernels, body(): pl.pallas_call(hand_out, out_shape=shapes, in_specs=[pl.BlockSpec(memory_...  19 us

profile of v2, /device:TPU:4, one launch (start us, length us, event | category | flops | bytes accessed | tf_op | source)
XLA Modules:
  0.0 102.5 jit_solution(12344507533083310024)
XLA Ops:
  0.6 82.8 %attention.1 = (bf16[128,1024]{1,0:T(8,128)(2,1)}, bf16[128,1024]{1,0:T(8,128)(2,1)}, bf16[128,128]{1,0:T(8,128)(2,1)}, bf16[128,128]{1,0:T(8,128)(2,1)}) custom-call(s32[4,128]{1,0:T(4,128)} %pos_ref.1, bf16[128,1024]{1,0:T(8,128)(2,1)} %bitcast.8, bf16[128,128]{1,0:T(8,128)(2,1)} %bitcast.10, bf16[128,128]{1,0:T(8,128)(2,1)} %bitcast.11, ...), custom_call_target="tpu_custom_call" | custom-call | tf_op jit(solution)/shard_map/attention/pallas_call | solution.py:698
  83.5 19.0 %hand_out.1 = (bf16[128,1024]{1,0:T(8,128)(2,1)}, bf16[128,1024]{1,0:T(8,128)(2,1)}, bf16[128,128]{1,0:T(8,128)(2,1)}, bf16[128,128]{1,0:T(8,128)(2,1)}) custom-call(bf16[128,1024]{1,0:T(8,128)(2,1)} %get-tuple-element.12.refs_0_, bf16[128,1024]{1,0:T(8,128)(2,1)} %get-tuple-element.13.refs_1_, bf16[128,128]{1,0:T(8,128)(2,1)} %get-tuple-element.14.refs_2_, ...), custom_call_target="tpu_custom_call" | custom-call | tf_op jit(solution)/shard_map/hand_out/pallas_call | solution.py:745

commit v3 on v2

--- a/solution.py
+++ b/solution.py
@@ -32,24 +32,26 @@
     return [(dy, dz) for dz in part]
 
 
-TABLE = [
-    a_chunk(0),
-    b_chunk(0, NEAR),
-    a_chunk(-1),
-    a_chunk(1),
-    b_chunk(0, FAR),
-    b_chunk(-1, NEAR),
-    b_chunk(1, NEAR),
-    a_chunk(-2),
-    a_chunk(2),
-    b_chunk(-1, FAR),
-    b_chunk(1, FAR),
-    a_chunk(-3),
-    a_chunk(3),
-    b_chunk(2, NEAR),
-    b_chunk(2, FAR),
-    a_chunk(4),
-]
+NAMES = (
+    ("A0", a_chunk(0)),
+    ("B0n", b_chunk(0, NEAR)),
+    ("A-1", a_chunk(-1)),
+    ("A+1", a_chunk(1)),
+    ("B+1n", b_chunk(1, NEAR)),
+    ("B0f", b_chunk(0, FAR)),
+    ("A-2", a_chunk(-2)),
+    ("A+2", a_chunk(2)),
+    ("B-1n", b_chunk(-1, NEAR)),
+    ("B+1f", b_chunk(1, FAR)),
+    ("A-3", a_chunk(-3)),
+    ("A+3", a_chunk(3)),
+    ("B2n", b_chunk(2, NEAR)),
+    ("B-1f", b_chunk(-1, FAR)),
+    ("B2f", b_chunk(2, FAR)),
+    ("A4", a_chunk(4)),
+)
+TABLE = [windows for _, windows in NAMES]
+AT = {name: number for number, (name, _) in enumerate(NAMES)}
 
 
 def nt(a, b):
@@ -100,6 +102,7 @@
     lse,
     mc,
     wt,
+    mot,
     pot,
     pd,
     xd,
@@ -187,48 +190,68 @@
     msg("ay2", buf.at[0, 0], buf.at[0, 2], ym)
     msg("ay3", buf.at[0, 1], buf.at[0, 3], yp)
     for w in range(4):
-        msg("azp%d" % w, buf.at[0, w], buf.at[2, w], zp)
-        msg("azm%d" % w, buf.at[0, w], buf.at[3, w], zm)
-        msg("byp%d" % w, buf.at[1, w], buf.at[5, w], yp)
-        msg("bym%d" % w, buf.at[1, w], buf.at[6, w], ym)
-    msg("a7", buf.at[2], buf.at[7], zp)
-    msg("a8", buf.at[3], buf.at[8], zm)
-    msg("a11", buf.at[7], buf.at[11], zp)
-    msg("a12", buf.at[8], buf.at[12], zm)
-    msg("a15p", buf.at[11, pl.ds(0, 2)], buf.at[15, pl.ds(0, 2)], zp)
-    msg("a15m", buf.at[12, pl.ds(2, 2)], buf.at[15, pl.ds(2, 2)], zm)
+        msg("azp%d" % w, buf.at[0, w], buf.at[AT["A-1"], w], zp)
+        msg("azm%d" % w, buf.at[0, w], buf.at[AT["A+1"], w], zm)
+        msg("byp%d" % w, buf.at[1, w], buf.at[AT["B-1n"], w], yp)
+        msg("bym%d" % w, buf.at[1, w], buf.at[AT["B+1n"], w], ym)
+
+    def block(name, source, target, first, count, dev):
+        span = pl.ds(first, count)
+        msg(name, buf.at[AT[source], span], buf.at[AT[target], span], dev)
+
+    block("a7a", "A-1", "A-2", 0, 3, zp)
+    block("a7b", "A-1", "A-2", 3, 1, zp)
+    block("a8a", "A+1", "A+2", 0, 3, zm)
+    block("a8b", "A+1", "A+2", 3, 1, zm)
+    block("a11a", "A-2", "A-3", 0, 2, zp)
+    block("a11b", "A-2", "A-3", 2, 2, zp)
+    block("a12a", "A+2", "A+3", 2, 2, zm)
+    block("a12b", "A+2", "A+3", 0, 2, zm)
+    block("a15p", "A-3", "A4", 0, 2, zp)
+    block("a15m", "A+3", "A4", 2, 2, zm)
+    far = AT["B0f"]
     msg("bz1", buf.at[1, 0], buf.at[1, 1], zp)
     msg("bz2", buf.at[1, 0], buf.at[1, 2], zm)
     msg("bz3", buf.at[1, 1], buf.at[1, 3], zp)
-    msg("bz4", buf.at[1, 2], buf.at[4, 0], zm)
-    msg("bz5", buf.at[1, 3], buf.at[4, 1], zp)
-    msg("bz6", buf.at[4, 0], buf.at[4, 2], zm)
-    msg("bz7", buf.at[4, 1], buf.at[4, 3], zp)
-    msg("b9", buf.at[4], buf.at[9], yp)
-    msg("b10", buf.at[4], buf.at[10], ym)
-    msg("b13", buf.at[5], buf.at[13], yp)
-    msg("b14", buf.at[10], buf.at[14], ym)
+    msg("bz4", buf.at[1, 2], buf.at[far, 0], zm)
+    msg("bz5", buf.at[1, 3], buf.at[far, 1], zp)
+    msg("bz6", buf.at[far, 0], buf.at[far, 2], zm)
+    msg("bz7", buf.at[far, 1], buf.at[far, 3], zp)
+    block("b9a", "B0f", "B-1f", 0, 3, yp)
+    block("b9b", "B0f", "B-1f", 3, 1, yp)
+    block("b10a", "B0f", "B+1f", 0, 3, ym)
+    block("b10b", "B0f", "B+1f", 3, 1, ym)
+    block("b13", "B-1n", "B2n", 0, 4, yp)
+    block("b14a", "B+1f", "B2f", 0, 3, ym)
+    block("b14b", "B+1f", "B2f", 3, 1, ym)
     for n, dev in enumerate((cp, xp, dp)):
         msg("stat%d" % n, stat, pstat.at[n], dev)
     for n, dev in enumerate((cp, xp, dp)):
-        msg("ot%d" % n, ot.at[n + 1], pot.at[n], dev)
+        msg("ot%d" % n, mot.at[n], pot.at[n], dev)
     msg("dq3", dqt.at[3], pd.at[0], cp)
     msg("dq2", xd, px, xp)
     msg("dq1", dqt.at[1], pd.at[1], cp)
-    msg("r15m", snd.at[15, pl.ds(0, 2)], r1.at[11, pl.ds(0, 2)], zm)
-    msg("r15p", snd.at[15, pl.ds(2, 2)], r1.at[12, pl.ds(2, 2)], zp)
-    msg("r11", snd.at[11], r1.at[7], zm)
-    msg("r12", snd.at[12], r1.at[8], zp)
-    msg("r7", snd.at[7], r1.at[2], zm)
-    msg("r8", snd.at[8], r1.at[3], zp)
-    msg("r2", snd.at[2], r1.at[0], zm)
-    msg("r3", snd.at[3], r2.at[0], zp)
-    msg("r13", snd.at[13], r1.at[5], ym)
-    msg("r14", snd.at[14], r1.at[10], yp)
-    msg("r5", snd.at[5], r1.at[1], ym)
-    msg("r9", snd.at[9], r1.at[4], ym)
-    msg("r6", snd.at[6], r2.at[1], yp)
-    msg("r10", snd.at[10], r2.at[2], yp)
+    def back(name, source, target, first, count, dev, into=None):
+        span = pl.ds(first, count)
+        into = r1.at[AT[target], span] if into is None else r2.at[into, span]
+        msg(name, snd.at[AT[source], span], into, dev)
+
+    back("rA4m", "A4", "A-3", 0, 2, zm)
+    back("rA4p", "A4", "A+3", 2, 2, zp)
+    back("rA-3", "A-3", "A-2", 0, 4, zm)
+    back("rA+3", "A+3", "A+2", 0, 4, zp)
+    back("rA-2", "A-2", "A-1", 0, 4, zm)
+    back("rA+2", "A+2", "A+1", 0, 4, zp)
+    back("rA-1a", "A-1", "A0", 2, 2, zm)
+    back("rA-1b", "A-1", "A0", 0, 2, zm)
+    back("rA+1a", "A+1", "A0", 2, 2, zp, 0)
+    back("rA+1b", "A+1", "A0", 0, 2, zp, 0)
+    back("rB2n", "B2n", "B-1n", 0, 4, ym)
+    back("rB2f", "B2f", "B+1f", 0, 4, yp)
+    back("rB-1n", "B-1n", "B0n", 0, 4, ym)
+    back("rB-1f", "B-1f", "B0f", 0, 4, ym)
+    back("rB+1n", "B+1n", "B0n", 0, 4, yp, 1)
+    back("rB+1f", "B+1f", "B0f", 0, 4, yp, 2)
     for n, dev in enumerate((ym, ym, yp)):
         msg("ry%d" % n, sy.at[n], ry.at[n], dev)
     for n, dev in enumerate((zm, zm, zm, zm, zp, zp, zp)):
@@ -237,7 +260,7 @@
     go("q2", "q1")
     for copy in pieces:
         copy.wait()
-    go("ay1", "ay2", "bz1", "bz2", "azp0", "azm0", "byp0", "bym0", "g2", "g1")
+    go("ay1", "ay2", "bz1", "bz2", "azp0", "azm0", "byp0", "bym0", "g1")
     fetch[0].wait()
 
     for p, (row, column) in enumerate(
@@ -280,16 +303,17 @@
     stat[2:8] = jnp.full((6, ROWS), NEG, jnp.float32)
     ls[2:8] = jnp.zeros((6, 8, ROWS), jnp.float32)
 
-    fetch[2].wait()
-    spread(0, mg, gn, gt)
     got("ay3", "bz3", "bz4")
     go("azp3", "azm3", "bz5", "bz6", "byp3", "bym3")
+    for w in range(3):
+        got("azp%d" % w, "azm%d" % w)
+    go("a7a", "a8a")
     for p in range(1, 4):
         ot[p] = jnp.zeros((2 * DIM, ROWS), jnp.float32)
-    for c in (6, 9, 13, 14, 15):
-        r1[c] = jnp.zeros((4, 4, HALF, DIM), jnp.bfloat16)
-    r1[11, 2:4] = jnp.zeros((2, 4, HALF, DIM), jnp.bfloat16)
-    r1[12, 0:2] = jnp.zeros((2, 4, HALF, DIM), jnp.bfloat16)
+    for name in ("B+1n", "B2n", "B-1f", "B2f", "A4"):
+        r1[AT[name]] = jnp.zeros((4, 4, HALF, DIM), jnp.bfloat16)
+    r1[AT["A-3"], 2:4] = jnp.zeros((2, 4, HALF, DIM), jnp.bfloat16)
+    r1[AT["A+3"], 0:2] = jnp.zeros((2, 4, HALF, DIM), jnp.bfloat16)
 
     def take(i, kind):
         return buf[pl.ds(2 * i, 2), :, kind].reshape(KEYS, DIM)
@@ -325,20 +349,26 @@
                 for step, names in steps:
                     step(*names)
 
-        quads = range(4)
-
         @pl.when(n == 1)
         def _():
+            got("azp3", "azm3", "bz5", "bz6")
+            go("a7b", "a8b", "bz7", "b9a", "b10a")
+            got("byp0", "byp1", "byp2", "byp3")
+            go("b13")
+            fetch[2].wait()
+            spread(0, mg, gn, gt)
             got("q2")
-            go("q3")
+            go("q3", "g2")
             spread(2, pq.at[1], qn, qt)
             got("q3")
             spread(3, pq.at[2], qn, qt)
 
-        do(2, (got, ["azp%d" % w for w in quads] + ["azm%d" % w for w in quads]), (go, ["a7", "a8"]))
-        do(2, (got, ["bz5", "bz6"]), (go, ["bz7"]))
-        do(4, (got, ["bz7"]), (go, ["b9", "b10"]), (got, ["byp%d" % w for w in quads]), (go, ["b13"]))
-        do(5, (got, ["g2"]), (go, ["g3"]))
+        do(2, (got, ["a7a", "a7b", "a8a", "a8b", "bz7"]))
+        do(2, (go, ["a11a", "a12a", "a11b", "a12b", "b9b", "b10b"]))
+        do(4, (got, ["bym%d" % w for w in range(4)] + ["b10a"]), (go, ["b14a"]))
+        do(6, (got, ["a11a", "a12a"]), (go, ["a15p", "a15m"]))
+        do(6, (got, ["b10b"]), (go, ["b14b"]))
+        do(7, (got, ["g2"]), (go, ["g3"]))
 
         @pl.when(n == 9)
         def _():
@@ -346,12 +376,9 @@
             for p in range(1, 4):
                 spread(p, pg.at[p - 1], gn, gt)
 
-        do(6, (got, ["bym%d" % w for w in quads] + ["a7", "a8"]), (go, ["a11", "a12"]))
-        do(8, (got, ["b9"]))
-        do(9, (got, ["b10"]), (go, ["b14"]))
-        do(10, (got, ["a11", "a12"]), (go, ["a15p", "a15m"]))
-        do(12, (got, ["b13"]))
-        do(14, (got, ["b14", "a15p", "a15m"]))
+        do(10, (got, ["a11b", "a12b"]))
+        do(12, (got, ["b13", "b9a", "b9b"]))
+        do(14, (got, ["b14a", "b14b", "a15p", "a15m"]))
 
     def forward(n, carry):
         arrive(n)
@@ -421,6 +448,8 @@
             rows = slice(lh * DIM, (lh + 1) * DIM)
             stat[16 + r : 17 + r] = row_sum(ot[p, rows] * gt[p, rows].astype(jnp.float32))
     go("stat2", "stat1", "stat0")
+    for n in range(3):
+        mot[n] = ot[n + 1].astype(jnp.bfloat16)
     go("ot0", "ot1", "ot2")
 
     dqt[1:4] = jnp.zeros((3, 2 * DIM, ROWS), jnp.float32)
@@ -462,7 +491,7 @@
 
     def b_total(dz, *arrived):
         got(*["rz%d" % n for n in arrived])
-        for slot, c in ((1, 1), (2, 4)):
+        for slot, c in ((1, 1), (2, far)):
             for w in range(4):
                 if TABLE[c][w][1] == dz:
                     return total_of(c, w, slot, rz, *arrived)
@@ -563,17 +592,24 @@
                     add(c)
                     go(*sends)
 
-        finish(7, (15, [], ["r15m", "r15p"]), (14, [], ["r14"]))
-        finish(6, (13, [], ["r13"]), (12, ["r15p"], ["r12"]))
-        finish(5, (11, ["r15m"], ["r11"]), (10, ["r14"], ["r10"]))
-        finish(4, (9, [], ["r9"]), (8, ["r12"], ["r8"]))
-        finish(3, (6, [], ["r6"]), (7, ["r11"], ["r7"]))
-        finish(2, (5, ["r13"], ["r5"]))
-        finish(1, (2, ["r7"], ["r2"]), (3, ["r8"], ["r3"]))
+        def step(name, waits=(), sends=None):
+            return AT[name], waits, ["r" + name] if sends is None else sends
+
+        finish(7, step("B2f"), step("A4", (), ["rA4m", "rA4p"]))
+        finish(6, step("B2n"), step("B-1f"))
+        finish(5, step("A-3", ["rA4m"]), step("A+3", ["rA4p"]))
+        finish(4, step("B-1n", ["rB2n"]), step("B+1f", ["rB2f"]))
+        finish(3, step("A-2", ["rA-3"]), step("A+2", ["rA+3"]))
+        finish(2, step("B+1n"))
+        finish(
+            1,
+            step("A-1", ["rA-2"], ["rA-1a", "rA-1b"]),
+            step("A+1", ["rA+2"], ["rA+1a", "rA+1b"]),
+        )
 
         @pl.when(n == 2 * (STEPS - 1 - 2) + 1)
         def _():
-            got("r9", "r10")
+            got("rB-1f", "rB+1f")
             chain(4, 0)
             chain(3, 4)
 
@@ -599,7 +635,7 @@
             rows = slice(lh * DIM, (lh + 1) * DIM)
             total = ot[0, rows] * lse[16 + lh : 17 + lh]
             for n in range(1, 4):
-                total = total + pot[n - 1, rows] * lse[16 + 2 * n + lh : 17 + 2 * n + lh]
+                total = total + pot[n - 1, rows].astype(jnp.float32) * lse[16 + 2 * n + lh : 17 + 2 * n + lh]
             halves.append(total)
         store(att_ref, jnp.concatenate(halves, axis=0).T.astype(jnp.bfloat16))
 
@@ -609,14 +645,13 @@
 
         @stage(0)
         def _():
-            got("r5", "r6")
+            got("rB-1n", "rB+1n")
             chain(-2, 2, 1)
             chain(1, 6, 5)
 
         @stage(1)
         def _():
-            attend()
-            got("r2", "r3")
+            got("rA-1a", "rA+1a")
             a_send(3, 0)
             a_send(2, 2)
 
@@ -626,8 +661,9 @@
 
         @stage(3)
         def _():
+            chain(-1, 3, 2)
+            got("rA-1b", "rA+1b")
             a_send(1, 1, 0)
-            chain(-1, 3, 2)
 
         @stage(4)
         def _():
@@ -638,6 +674,7 @@
         @stage(6)
         def _():
             go("dq1")
+            attend()
 
         p = 3 - n // 2
         lows, cats, d1, d2 = [], [], [], []
@@ -672,15 +709,8 @@
 
 
 def hand_out(*refs):
-    sources, targets, sems = refs[:4], refs[4:8], refs[8]
-    copies = [
-        pltpu.make_async_copy(src, dst, sems.at[n])
-        for n, (src, dst) in enumerate(zip(sources, targets))
-    ]
-    for copy in copies:
-        copy.start()
-    for copy in copies:
-        copy.wait()
+    for source, target in zip(refs[:4], refs[4:]):
+        target[...] = source[...]
 
 
 def body(queries, keys, values, grad_out, block_pos):
@@ -688,7 +718,7 @@
     bf, f32 = jnp.bfloat16, jnp.float32
     window = (4, HALF, DIM)
     raw = (2 * BLK, HEADS * DIM)
-    count = 80
+    count = 96
     shapes = [
         jax.ShapeDtypeStruct(raw, bf),
         jax.ShapeDtypeStruct(raw, bf),
@@ -718,7 +748,8 @@
             pltpu.VMEM((24, ROWS), f32),
             pltpu.VMEM((STEPS, 8, ROWS), f32),
             pltpu.VMEM((STEPS, 4, 2, KEYS, ROWS), bf),
-            pltpu.VMEM((3, 2 * DIM, ROWS), f32),
+            pltpu.VMEM((3, 2 * DIM, ROWS), bf),
+            pltpu.VMEM((3, 2 * DIM, ROWS), bf),
             pltpu.VMEM((2, 2 * DIM, ROWS), f32),
             pltpu.VMEM((2 * DIM, ROWS), bf),
             pltpu.VMEM((2 * DIM, ROWS), bf),
@@ -745,9 +776,10 @@
     outs = pl.pallas_call(
         hand_out,
         out_shape=shapes,
-        in_specs=[pl.BlockSpec(memory_space=pl.ANY)] * 4,
-        out_specs=[pl.BlockSpec(memory_space=pltpu.HBM)] * 4,
-        scratch_shapes=[pltpu.SemaphoreType.DMA((4,))],
+        in_specs=[pl.BlockSpec(one.shape, lambda n: (0, 0)) for one in shapes],
+        out_specs=[pl.BlockSpec(one.shape, lambda n: (0, 0)) for one in shapes],
+        grid=(1,),
+        compiler_params=pltpu.CompilerParams(vmem_limit_bytes=54 * 1024 * 1024),
         name="hand_out",
     )(*outs)
     return tuple(out[None] for out in outs)

time: 103 us -> 85.7 us (0.83)
  Pallas kernels: 102 us -> 84.3 us
    pallas_call x1, Pallas kernels: 19 us -> 1.85 us  [body(): pl.pallas_call(hand_out, out_shape=shapes, in_specs=[pl.BlockSpec(one.sha...]
where the time goes in v3:
time: 85.7 us; the launch traced here: 84.9 us
  Pallas kernels  84.3 us (98%)
    pallas_call x1, Pallas kernels, body(): pl.pallas_call(kernel, out_shape=shapes, in_specs=[pl.BlockSpec(memory_sp...  82.4 us
    pallas_call x1, Pallas kernels, body(): pl.pallas_call(hand_out, out_shape=shapes, in_specs=[pl.BlockSpec(one.sha...  1.85 us

profile of v3, /device:TPU:4, one launch (start us, length us, event | category | flops | bytes accessed | tf_op | source)
XLA Modules:
  0.0 84.9 jit_solution(14550242203167655026)
XLA Ops:
  0.6 82.4 %attention.1 = (bf16[128,1024]{1,0:T(8,128)(2,1)}, bf16[128,1024]{1,0:T(8,128)(2,1)}, bf16[128,128]{1,0:T(8,128)(2,1)}, bf16[128,128]{1,0:T(8,128)(2,1)}) custom-call(s32[4,128]{1,0:T(4,128)} %pos_ref.1, bf16[128,1024]{1,0:T(8,128)(2,1)} %bitcast.8, bf16[128,128]{1,0:T(8,128)(2,1)} %bitcast.10, bf16[128,128]{1,0:T(8,128)(2,1)} %bitcast.11, ...), custom_call_target="tpu_custom_call" | custom-call | tf_op jit(solution)/shard_map/attention/pallas_call | solution.py:728
  83.0 1.9 %hand_out.1 = (bf16[128,1024]{1,0:T(8,128)(2,1)}, bf16[128,1024]{1,0:T(8,128)(2,1)}, bf16[128,128]{1,0:T(8,128)(2,1)}, bf16[128,128]{1,0:T(8,128)(2,1)}) custom-call(bf16[128,1024]{1,0:T(8,128)(2,1)} %get-tuple-element.12.refs_0_, bf16[128,1024]{1,0:T(8,128)(2,1)} %get-tuple-element.13.refs_1_, bf16[128,128]{1,0:T(8,128)(2,1)} %get-tuple-element.14.refs_2_, ...), custom_call_target="tpu_custom_call" | custom-call | tf_op jit(solution)/shard_map/hand_out/pallas_call | solution.py:776

commit v4 on v3

--- a/solution.py
+++ b/solution.py
@@ -14,8 +14,10 @@
 HEADS = 8
 ROWS = BLK * HEADS
 CHUNKS = 16
-STEPS = 8
-KEYS = 8 * HALF
+STEPS = 4
+BACK_STEPS = 8
+KEYS = 16 * HALF
+BACK_KEYS = 8 * HALF
 SCALE = DIM**-0.5
 C2 = SCALE * 1.4426950408889634
 
@@ -45,9 +47,9 @@
     ("B+1f", b_chunk(1, FAR)),
     ("A-3", a_chunk(-3)),
     ("A+3", a_chunk(3)),
+    ("B2f", b_chunk(2, FAR)),
+    ("B-1f", b_chunk(-1, FAR)),
     ("B2n", b_chunk(2, NEAR)),
-    ("B-1f", b_chunk(-1, FAR)),
-    ("B2f", b_chunk(2, FAR)),
     ("A4", a_chunk(4)),
 )
 TABLE = [windows for _, windows in NAMES]
@@ -81,6 +83,10 @@
     k_ref,
     v_ref,
     g_ref,
+    att_out,
+    dq_out,
+    dk_out,
+    dv_out,
     att_ref,
     dq_ref,
     dk_ref,
@@ -104,6 +110,7 @@
     wt,
     mot,
     pot,
+    sd,
     pd,
     xd,
     px,
@@ -184,8 +191,10 @@
 
     for name, src, dst in (("q", q_ref, pq), ("g", g_ref, pg)):
         msg(name + "1", src, dst.at[0], cp)
-        msg(name + "2", src, dst.at[1], xp)
-        msg(name + "3", dst.at[1], dst.at[2], cp)
+        for half in range(2):
+            span = pl.ds(half * BLK, BLK)
+            msg("%s2%d" % (name, half), src.at[span], dst.at[1, span], xp)
+            msg("%s3%d" % (name, half), dst.at[1, span], dst.at[2, span], cp)
     msg("ay1", buf.at[0, 0], buf.at[0, 1], yp)
     msg("ay2", buf.at[0, 0], buf.at[0, 2], ym)
     msg("ay3", buf.at[0, 1], buf.at[0, 3], yp)
@@ -228,9 +237,10 @@
         msg("stat%d" % n, stat, pstat.at[n], dev)
     for n, dev in enumerate((cp, xp, dp)):
         msg("ot%d" % n, mot.at[n], pot.at[n], dev)
-    msg("dq3", dqt.at[3], pd.at[0], cp)
-    msg("dq2", xd, px, xp)
-    msg("dq1", dqt.at[1], pd.at[1], cp)
+    for lh in range(2):
+        msg("dq3%d" % lh, sd.at[lh], pd.at[lh], cp)
+        msg("dq2%d" % lh, xd.at[lh], px.at[lh], xp)
+    msg("dq1", sd.at[pl.ds(2, 2)], pd.at[pl.ds(2, 2)], cp)
     def back(name, source, target, first, count, dev, into=None):
         span = pl.ds(first, count)
         into = r1.at[AT[target], span] if into is None else r2.at[into, span]
@@ -238,26 +248,30 @@
 
     back("rA4m", "A4", "A-3", 0, 2, zm)
     back("rA4p", "A4", "A+3", 2, 2, zp)
-    back("rA-3", "A-3", "A-2", 0, 4, zm)
-    back("rA+3", "A+3", "A+2", 0, 4, zp)
-    back("rA-2", "A-2", "A-1", 0, 4, zm)
-    back("rA+2", "A+2", "A+1", 0, 4, zp)
-    back("rA-1a", "A-1", "A0", 2, 2, zm)
-    back("rA-1b", "A-1", "A0", 0, 2, zm)
-    back("rA+1a", "A+1", "A0", 2, 2, zp, 0)
-    back("rA+1b", "A+1", "A0", 0, 2, zp, 0)
-    back("rB2n", "B2n", "B-1n", 0, 4, ym)
-    back("rB2f", "B2f", "B+1f", 0, 4, yp)
-    back("rB-1n", "B-1n", "B0n", 0, 4, ym)
-    back("rB-1f", "B-1f", "B0f", 0, 4, ym)
-    back("rB+1n", "B+1n", "B0n", 0, 4, yp, 1)
-    back("rB+1f", "B+1f", "B0f", 0, 4, yp, 2)
+    for half in range(2):
+        span = 2 * half, 2
+
+        def both(source, target, dev, into=None):
+            back("r%s%d" % (source, half), source, target, *span, dev, into)
+
+        both("A-3", "A-2", zm)
+        both("A+3", "A+2", zp)
+        both("A-2", "A-1", zm)
+        both("A+2", "A+1", zp)
+        both("A-1", "A0", zm)
+        both("A+1", "A0", zp, 0)
+        both("B2n", "B-1n", ym)
+        both("B2f", "B+1f", yp)
+        both("B-1n", "B0n", ym)
+        both("B-1f", "B0f", ym)
+        both("B+1n", "B0n", yp, 1)
+        both("B+1f", "B0f", yp, 2)
     for n, dev in enumerate((ym, ym, yp)):
         msg("ry%d" % n, sy.at[n], ry.at[n], dev)
     for n, dev in enumerate((zm, zm, zm, zm, zp, zp, zp)):
         msg("rz%d" % n, sz.at[n], rz.at[n], dev)
 
-    go("q2", "q1")
+    go("q20", "q21", "q1")
     for copy in pieces:
         copy.wait()
     go("ay1", "ay2", "bz1", "bz2", "azp0", "azm0", "byp0", "bym0", "g1")
@@ -315,16 +329,24 @@
     r1[AT["A-3"], 2:4] = jnp.zeros((2, 4, HALF, DIM), jnp.bfloat16)
     r1[AT["A+3"], 0:2] = jnp.zeros((2, 4, HALF, DIM), jnp.bfloat16)
 
-    def take(i, kind):
-        return buf[pl.ds(2 * i, 2), :, kind].reshape(KEYS, DIM)
-
-    def picks(i, p):
-        number = [kt[8 * i + w] for w in range(8)]
+    got("azp3", "azm3", "bz5", "bz6")
+    go("a7b", "a8b", "bz7", "b9a", "b10a")
+    got("byp0", "byp1", "byp2", "byp3")
+    go("b13")
+    got("q20")
+    go("q30")
+    fetch[2].wait()
+    spread(0, mg, gn, gt)
+    def take(first, count, kind):
+        return buf[pl.ds(first, count), :, kind].reshape(count * 4 * HALF, DIM)
+
+    def picks(first, count, p):
+        number = [kt[4 * first + w] for w in range(4 * count)]
         mine = kt[4 * CHUNKS + p]
         return [n < mine for n in number], [n == mine for n in number]
 
     def windows(x):
-        return [x[w * HALF : (w + 1) * HALF] for w in range(8)]
+        return [x[w * HALF : (w + 1) * HALF] for w in range(x.shape[0] // HALF)]
 
     def cat(low, high, chosen):
         zero = jnp.zeros((HALF, DIM), jnp.bfloat16)
@@ -335,8 +357,8 @@
             )
         return jnp.concatenate(rows, axis=0)
 
-    neg_rows = jnp.full((8, ROWS // 2), NEG, jnp.float32)
-    big_row = jnp.full((1, ROWS // 2), BIG, jnp.float32)
+    neg_rows = jnp.full((8, ROWS), NEG, jnp.float32)
+    big_row = jnp.full((1, ROWS), BIG, jnp.float32)
     high = slice(DIM, 2 * DIM)
 
     def row(ref, r):
@@ -351,66 +373,56 @@
 
         @pl.when(n == 1)
         def _():
-            got("azp3", "azm3", "bz5", "bz6")
-            go("a7b", "a8b", "bz7", "b9a", "b10a")
-            got("byp0", "byp1", "byp2", "byp3")
-            go("b13")
-            fetch[2].wait()
-            spread(0, mg, gn, gt)
-            got("q2")
-            go("q3", "g2")
+            got("q21")
+            go("q31", "g20", "g21")
             spread(2, pq.at[1], qn, qt)
-            got("q3")
+            got("q30", "q31")
             spread(3, pq.at[2], qn, qt)
-
-        do(2, (got, ["a7a", "a7b", "a8a", "a8b", "bz7"]))
-        do(2, (go, ["a11a", "a12a", "a11b", "a12b", "b9b", "b10b"]))
-        do(4, (got, ["bym%d" % w for w in range(4)] + ["b10a"]), (go, ["b14a"]))
-        do(6, (got, ["a11a", "a12a"]), (go, ["a15p", "a15m"]))
-        do(6, (got, ["b10b"]), (go, ["b14b"]))
-        do(7, (got, ["g2"]), (go, ["g3"]))
-
-        @pl.when(n == 9)
+            got("a7a", "a8a", "bz7")
+            go("b9b", "b10b")
+
+        do(2, (got, ["a7b", "a8b"]), (go, ["a11a", "a12a", "a11b", "a12b"]))
+        do(2, (got, ["bym%d" % w for w in range(4)] + ["b10a"]), (go, ["b14a"]))
+        do(3, (got, ["b10b"]), (go, ["b14b"]))
+        do(4, (got, ["a11a", "a12a"]), (go, ["a15p", "a15m"]))
+        do(4, (got, ["g20", "g21"]), (go, ["g30", "g31"]), (got, ["a11b", "a12b"]))
+        do(6, (got, ["b14a", "b14b", "b9a", "b9b", "b13", "a15p", "a15m"]))
+
+        @pl.when(n == 5)
         def _():
-            got("g1", "g3")
+            got("g1", "g30", "g31")
             for p in range(1, 4):
                 spread(p, pg.at[p - 1], gn, gt)
 
-        do(10, (got, ["a11b", "a12b"]))
-        do(12, (got, ["b13", "b9a", "b9b"]))
-        do(14, (got, ["b14a", "b14b", "a15p", "a15m"]))
-
     def forward(n, carry):
+        i, pair = n // 2, n % 2
         arrive(n)
-        i = n // 2
-        kl, kh, vl, vh = [take(i, kind) for kind in range(4)]
+        kl, kh, vl, vh = [take(4 * i, 4, kind) for kind in range(4)]
         parts = []
-        for unrolled in range(2):
-            p = 2 * (n % 2) + unrolled
-            low, same = picks(i, p)
+        for p in (2 * pair, 2 * pair + 1):
+            low, same = picks(4 * i, 4, p)
             kcat, vcat = cat(kl, kh, low), cat(vl, vh, low)
-            for lanes in (slice(0, ROWS // 2), slice(ROWS // 2, ROWS)):
-                olds = [stat[pl.ds(2 * p + lh, 1), lanes] for lh in range(2)]
-                parts.append((p, lanes, low, same, kcat, vcat, olds))
+            olds = [row(stat, 2 * p + lh) for lh in range(2)]
+            parts.append((p, low, same, kcat, vcat, olds))
 
         def scores(part):
-            p, lanes, _, _, kcat, _, _ = part
-            return nt(kl, qt[p, high, lanes]), windows(nt(kcat, qt[p, :, lanes]))
+            p, _, _, kcat, _, _ = part
+            return nt(kl, qt[p, high]), windows(nt(kcat, qt[p]))
 
         def weigh(part, s1, s2):
-            p, lanes, low, same, _, vcat, (ml, mh) = part
+            p, low, same, _, vcat, (ml, mh) = part
             rl, rh = 2 * p, 2 * p + 1
             tops_l, tops_h = neg_rows, fold(s1, jnp.max)
-            for w in range(8):
+            for w in range(16):
                 top = fold(s2[w], jnp.max)
                 tops_l = jnp.maximum(tops_l, lax.select(low[w], top, neg_rows))
                 tops_h = jnp.maximum(tops_h, lax.select(low[w] | same[w], neg_rows, top))
             nl, nh = jnp.maximum(ml, row_max(tops_l)), jnp.maximum(mh, row_max(tops_h))
             fl, fh = jnp.exp2((ml - nl) * C2), jnp.exp2((mh - nh) * C2)
             p1 = jnp.exp2((s1 - nh) * C2)
-            tl, th = ls[rl, :, lanes] * fl, ls[rh, :, lanes] * fh + fold(p1, jnp.sum)
+            tl, th = ls[rl] * fl, ls[rh] * fh + fold(p1, jnp.sum)
             pieces = []
-            for w in range(8):
+            for w in range(16):
                 ref = lax.select(same[w], big_row, lax.select(low[w], nl, nh))
                 piece = jnp.exp2((s2[w] - ref) * C2)
                 total = fold(piece, jnp.sum)
@@ -418,20 +430,21 @@
                 tl = tl + lax.select(low[w], total, zero)
                 th = th + lax.select(low[w], zero, total)
                 pieces.append(piece.astype(jnp.bfloat16))
-            ls[rl, :, lanes], ls[rh, :, lanes] = tl, th
-            stat[pl.ds(rl, 1), lanes], stat[pl.ds(rh, 1), lanes] = nl, nh
-            mc[i, pl.ds(rl, 1), lanes], mc[i, pl.ds(rh, 1), lanes] = nl, nh
+            ls[rl], ls[rh] = tl, th
+            stat[pl.ds(rl, 1)], stat[pl.ds(rh, 1)] = nl, nh
+            mc[i, pl.ds(rl, 1)], mc[i, pl.ds(rh, 1)] = nl, nh
             w1, w2 = p1.astype(jnp.bfloat16), jnp.concatenate(pieces, axis=0)
-            wt[i, p, 0, :, lanes], wt[i, p, 1, :, lanes] = w1, w2
-            return p, lanes, fl, fh, tn(vl, w1), tn(vcat, w2)
-
-        def update(p, lanes, fl, fh, o1, o2):
-            ot[p, 0:DIM, lanes] = ot[p, 0:DIM, lanes] * fl + o2[0:DIM]
-            ot[p, high, lanes] = ot[p, high, lanes] * fh + (o1 + o2[high])
+            wt[i, p, 0], wt[i, p, 1] = w1, w2
+            return p, fl, fh, w1, w2, vcat
+
+        def update(p, fl, fh, w1, w2, vcat):
+            o1, o2 = tn(vl, w1), tn(vcat, w2)
+            ot[p, 0:DIM] = ot[p, 0:DIM] * fl + o2[0:DIM]
+            ot[p, high] = ot[p, high] * fh + (o1 + o2[high])
 
         now, late = scores(parts[0]), None
-        for k in range(4):
-            later = scores(parts[k + 1]) if k < 3 else None
+        for k in range(2):
+            later = scores(parts[k + 1]) if k < 1 else None
             done = weigh(parts[k], *now)
             if late is not None:
                 update(*late)
@@ -453,6 +466,9 @@
     go("ot0", "ot1", "ot2")
 
     dqt[1:4] = jnp.zeros((3, 2 * DIM, ROWS), jnp.float32)
+    early = [name for name in msgs if name[0] in "qgab"]
+    for name in early:
+        msgs[name].wait_send()
     got("stat0", "stat1", "stat2")
     for p in range(4):
         for lh in range(2):
@@ -509,40 +525,42 @@
         go("ry%d" % leaving)
 
     def backward(n, carry):
-        i = STEPS - 1 - n // 2
-        vl, vh = take(i, 2), take(i, 3)
+        i = BACK_STEPS - 1 - n
+        step, rows = i // 2, pl.ds((i % 2) * BACK_KEYS, BACK_KEYS)
+        kl, kh, vl, vh = [take(2 * i, 2, kind) for kind in range(4)]
         parts = []
-        for unrolled in range(2):
-            p = 2 * (n % 2) + unrolled
-            low, same = picks(i, p)
-            vcat = cat(vl, vh, low)
-            for lanes in (slice(0, ROWS // 2), slice(ROWS // 2, ROWS)):
-                parts.append((p, lanes, low, vcat))
+        for p in range(4):
+            low, same = picks(2 * i, 2, p)
+            parts.append((p, low, cat(vl, vh, low)))
 
         def dots(part):
-            p, lanes, _, vcat = part
-            return nt(vl, gt[p, high, lanes]), windows(nt(vcat, gt[p, :, lanes]))
+            p, _, vcat = part
+            return nt(vl, gt[p, high]), windows(nt(vcat, gt[p]))
 
         def work(part, g1, g2):
-            p, lanes, low, _ = part
+            p, low, _ = part
             rl, rh = 2 * p, 2 * p + 1
-            el, eh = lse[pl.ds(8 + rl, 1), lanes], lse[pl.ds(8 + rh, 1), lanes]
-            fl = jnp.exp2((mc[i, pl.ds(rl, 1), lanes] - lse[pl.ds(rl, 1), lanes]) * C2)
-            fh = jnp.exp2((mc[i, pl.ds(rh, 1), lanes] - lse[pl.ds(rh, 1), lanes]) * C2)
-            p1 = wt[i, p, 0, :, lanes].astype(jnp.float32) * fh
+            el, eh = lse[8 + rl : 9 + rl], lse[8 + rh : 9 + rh]
+            fl = jnp.exp2((mc[step, rl : rl + 1] - lse[rl : rl + 1]) * C2)
+            fh = jnp.exp2((mc[step, rh : rh + 1] - lse[rh : rh + 1]) * C2)
+            p1 = wt[step, p, 0, rows].astype(jnp.float32) * fh
             ds1 = (p1 * (g1 - eh)).astype(jnp.bfloat16)
-            w2 = windows(wt[i, p, 1, :, lanes].astype(jnp.float32))
+            w2 = windows(wt[step, p, 1, rows].astype(jnp.float32))
             ps, ds = [], []
             for w in range(8):
                 piece = w2[w] * lax.select(low[w], fl, fh)
                 ps.append(piece.astype(jnp.bfloat16))
                 ds.append((piece * (g2[w] - lax.select(low[w], el, eh))).astype(jnp.bfloat16))
             p2, ds2 = jnp.concatenate(ps, axis=0), jnp.concatenate(ds, axis=0)
-            wt[i, p, 0, :, lanes], wt[i, p, 1, :, lanes] = ds1, ds2
-            return p1.astype(jnp.bfloat16), ds1, p2, ds2
-
-        def products(p, low, left, right):
-            p1, ds1, p2, ds2 = [jnp.concatenate([a, b], axis=1) for a, b in zip(left, right)]
+            if p < 2:
+                wt[step, p, 0, rows], wt[step, p, 1, rows] = ds1, ds2
+            if p >= 2:
+                one, two = tn(kl, ds1), tn(cat(kl, kh, low), ds2)
+                dqt[p, 0:DIM] = dqt[p, 0:DIM] + two[0:DIM]
+                dqt[p, high] = dqt[p, high] + (one + two[high])
+            return p, low, p1.astype(jnp.bfloat16), ds1, p2, ds2
+
+        def products(sums, p, low, p1, ds1, p2, ds2):
             new = []
             for one, two in (
                 (nt(ds1, qn[p, :, high]), nt(ds2, qn[p])),
@@ -551,82 +569,78 @@
                 zero = jnp.zeros((HALF, DIM), jnp.float32)
                 lows, highs = [], []
                 for w in range(8):
-                    rows = slice(w * HALF, (w + 1) * HALF)
-                    lows.append(one[rows] + lax.select(low[w], two[rows, 0:DIM], zero))
-                    highs.append(lax.select(low[w], zero, two[rows, high]))
+                    here = slice(w * HALF, (w + 1) * HALF)
+                    lows.append(one[here] + lax.select(low[w], two[here, 0:DIM], zero))
+                    highs.append(lax.select(low[w], zero, two[here, high]))
                 new += [lows, highs]
-            return new
-
-        dot0, dot1 = dots(parts[0]), dots(parts[1])
-        work0 = work(parts[0], *dot0)
-        dot2 = dots(parts[2])
-        work1 = work(parts[1], *dot1)
-        dot3 = dots(parts[3])
-        sums = products(parts[0][0], parts[0][2], work0, work1)
-        work2 = work(parts[2], *dot2)
-        work3 = work(parts[3], *dot3)
-        others = products(parts[2][0], parts[2][2], work2, work3)
-        sums = [[a + b for a, b in zip(x, y)] for x, y in zip(sums, others)]
-
-        @pl.when(n % 2 == 0)
+            if sums is None:
+                return new
+            return [[a + b for a, b in zip(x, y)] for x, y in zip(sums, new)]
+
+        sums, late = None, None
+        now = dots(parts[0])
+        for k in range(4):
+            later = dots(parts[k + 1]) if k < 3 else None
+            done = work(parts[k], *now)
+            if late is not None:
+                sums = products(sums, *late)
+            now, late = later, done
+        sums = products(sums, *late)
+        for kind in range(4):
+            for w in range(8):
+                tf[2 * i + w // 4, w % 4, kind] = sums[kind][w]
+
+        def finish(at_step, *chunks):
+            @pl.when(i == at_step)
+            def _():
+                for name, waits in chunks:
+                    for half in (1, 0) if name in ("A-1", "A+1") else (0, 1):
+                        c, span = AT[name], pl.ds(2 * half, 2)
+                        if waits[half]:
+                            got(waits[half])
+                        total = tf[c, span] + r1[c, span].astype(jnp.float32)
+                        snd[c, span] = total.astype(jnp.bfloat16)
+                        go(("rA4m", "rA4p")[half] if name == "A4" else "r%s%d" % (name, half))
+
+        def upstream(name):
+            return ["r%s%d" % (name, half) for half in range(2)]
+
+        none = [None, None]
+        finish(7, ("A4", none), ("B2n", none))
+        finish(6, ("B2f", none), ("B-1f", none))
+        finish(5, ("A-3", ["rA4m", None]), ("A+3", [None, "rA4p"]))
+        finish(4, ("B-1n", upstream("B2n")), ("B+1f", upstream("B2f")))
+        finish(3, ("A-2", upstream("A-3")), ("A+2", upstream("A+3")))
+        finish(2, ("B+1n", none))
+        finish(1, ("A-1", upstream("A-2")), ("A+1", upstream("A+2")))
+
+        @pl.when(i == 2)
         def _():
-            for kind in range(4):
-                for w in range(8):
-                    tf[2 * i + w // 4, w % 4, kind] = sums[kind][w]
-
-        @pl.when(n % 2 == 1)
-        def _():
-            for kind in range(4):
-                for w in range(8):
-                    at_chunk = 2 * i + w // 4
-                    tf[at_chunk, w % 4, kind] = tf[at_chunk, w % 4, kind] + sums[kind][w]
-
-        def add(c):
-            snd[c] = (tf[c] + r1[c].astype(jnp.float32)).astype(jnp.bfloat16)
-
-        def finish(at_step, *chunks):
-            @pl.when(n == 2 * (STEPS - 1 - at_step) + 1)
-            def _():
-                for c, waits, sends in chunks:
-                    got(*waits)
-                    add(c)
-                    go(*sends)
-
-        def step(name, waits=(), sends=None):
-            return AT[name], waits, ["r" + name] if sends is None else sends
-
-        finish(7, step("B2f"), step("A4", (), ["rA4m", "rA4p"]))
-        finish(6, step("B2n"), step("B-1f"))
-        finish(5, step("A-3", ["rA4m"]), step("A+3", ["rA4p"]))
-        finish(4, step("B-1n", ["rB2n"]), step("B+1f", ["rB2f"]))
-        finish(3, step("A-2", ["rA-3"]), step("A+2", ["rA+3"]))
-        finish(2, step("B+1n"))
-        finish(
-            1,
-            step("A-1", ["rA-2"], ["rA-1a", "rA-1b"]),
-            step("A+1", ["rA+2"], ["rA+1a", "rA+1b"]),
-        )
-
-        @pl.when(n == 2 * (STEPS - 1 - 2) + 1)
-        def _():
-            got("rB-1f", "rB+1f")
+            got("rB-1f0", "rB-1f1", "rB+1f0", "rB+1f1")
             chain(4, 0)
             chain(3, 4)
 
-        @pl.when(n == 2 * (STEPS - 1 - 1) + 1)
+        @pl.when(i == 1)
         def _():
             chain(-3, 1, 0)
             chain(2, 5, 4)
 
         return carry
 
-    lax.fori_loop(0, 2 * STEPS, backward, 0)
+    lax.fori_loop(0, BACK_STEPS, backward, 0)
 
     def store(ref, rows):
         for h in range(HEADS):
             lanes = slice(h * DIM, (h + 1) * DIM)
             ref[0:BLK, lanes] = rows[h * BLK : (h + 1) * BLK, 0:DIM]
             ref[BLK : 2 * BLK, lanes] = rows[h * BLK : (h + 1) * BLK, DIM : 2 * DIM]
+
+    leave = [
+        pltpu.make_async_copy(src, dst, lsem.at[11 + n])
+        for n, (src, dst) in enumerate(
+            ((att_ref, att_out), (dq_ref, dq_out), (dk_ref, dk_out), (dv_ref, dv_out))
+        )
+    ]
 
     def attend():
         got("ot0", "ot1", "ot2")
@@ -639,49 +653,45 @@
             halves.append(total)
         store(att_ref, jnp.concatenate(halves, axis=0).T.astype(jnp.bfloat16))
 
+    for lh in range(2):
+        sd[lh] = dqt[3, lh * DIM : (lh + 1) * DIM].astype(jnp.bfloat16)
+        go("dq3%d" % lh)
+    got("rB-1n0", "rB-1n1", "rB+1n0", "rB+1n1")
+    chain(-2, 2, 1)
+    chain(1, 6, 5)
+    attend()
+    leave[0].start()
+    for lh in range(2):
+        got("dq3%d" % lh)
+        part = dqt[2, lh * DIM : (lh + 1) * DIM] + pd[lh].astype(jnp.float32)
+        xd[lh] = part.astype(jnp.bfloat16)
+        go("dq2%d" % lh)
+
     def queries_back(n, carry):
         def stage(at_step):
             return pl.when(n == at_step)
 
         @stage(0)
         def _():
-            got("rB-1n", "rB+1n")
-            chain(-2, 2, 1)
-            chain(1, 6, 5)
-
-        @stage(1)
-        def _():
-            got("rA-1a", "rA+1a")
+            got("rA-11", "rA+11")
             a_send(3, 0)
             a_send(2, 2)
 
         @stage(2)
         def _():
-            go("dq3")
-
-        @stage(3)
-        def _():
+            for lh in range(2):
+                sd[2 + lh] = dqt[1, lh * DIM : (lh + 1) * DIM].astype(jnp.bfloat16)
+            go("dq1")
             chain(-1, 3, 2)
-            got("rA-1b", "rA+1b")
+            got("rA-10", "rA+10")
             a_send(1, 1, 0)
 
-        @stage(4)
-        def _():
-            got("dq3")
-            xd[...] = (dqt[2] + pd[0]).astype(jnp.bfloat16)
-            go("dq2")
-
-        @stage(6)
-        def _():
-            go("dq1")
-            attend()
-
-        p = 3 - n // 2
+        p = 1 - n // 2
         lows, cats, d1, d2 = [], [], [], []
-        for k in range(4):
-            i = 4 * (n % 2) + k
-            kl, kh = take(i, 0), take(i, 1)
-            low, same = picks(i, p)
+        for k in range(2):
+            i = 2 * (n % 2) + k
+            kl, kh = take(4 * i, 4, 0), take(4 * i, 4, 1)
+            low, same = picks(4 * i, 4, p)
             lows.append(kl)
             cats.append(cat(kl, kh, low))
             d1.append(wt[i, p, 0])
@@ -692,7 +702,7 @@
         dqt[p, high] = dqt[p, high] + (one + two[high])
         return carry
 
-    lax.fori_loop(0, 8, queries_back, 0)
+    lax.fori_loop(0, 4, queries_back, 0)
 
     for half, total in enumerate((a_total(0, 1, 2), b_total(0, 3, 6))):
         total = total + dg[half]
@@ -701,11 +711,20 @@
             dk_ref[rows, :] = (total[lh] * SCALE).astype(jnp.bfloat16)
             dv_ref[rows, :] = total[2 + lh].astype(jnp.bfloat16)
 
-    got("dq2", "dq1")
-    total = dqt[0] + pd[1] + px[...].astype(jnp.float32)
-    store(dq_ref, (total * SCALE).T.astype(jnp.bfloat16))
-    for copy in msgs.values():
-        copy.wait_send()
+    leave[2].start()
+    leave[3].start()
+    got("dq1", "dq20", "dq21")
+    halves = []
+    for lh in range(2):
+        part = dqt[0, lh * DIM : (lh + 1) * DIM] + pd[2 + lh].astype(jnp.float32)
+        halves.append(part + px[lh].astype(jnp.float32))
+    store(dq_ref, (jnp.concatenate(halves, axis=0) * SCALE).T.astype(jnp.bfloat16))
+    leave[1].start()
+    for name, copy in msgs.items():
+        if name not in early:
+            copy.wait_send()
+    for copy in leave:
+        copy.wait()
 
 
 def hand_out(*refs):
@@ -714,11 +733,10 @@
 
 
 def body(queries, keys, values, grad_out, block_pos):
-    vmem = pl.BlockSpec(memory_space=pltpu.VMEM)
     bf, f32 = jnp.bfloat16, jnp.float32
     window = (4, HALF, DIM)
     raw = (2 * BLK, HEADS * DIM)
-    count = 96
+    count = 108
     shapes = [
         jax.ShapeDtypeStruct(raw, bf),
         jax.ShapeDtypeStruct(raw, bf),
@@ -729,8 +747,12 @@
         kernel,
         out_shape=shapes,
         in_specs=[pl.BlockSpec(memory_space=pltpu.HBM)] * 5,
-        out_specs=[vmem] * 4,
+        out_specs=[pl.BlockSpec(memory_space=pltpu.HBM)] * 4,
         scratch_shapes=[
+            pltpu.VMEM(raw, bf),
+            pltpu.VMEM(raw, bf),
+            pltpu.VMEM((2 * BLK, DIM), bf),
+            pltpu.VMEM((2 * BLK, DIM), bf),
             pltpu.VMEM((CHUNKS, 4) + window, bf),
             pltpu.VMEM(raw, bf),
             pltpu.VMEM(raw, bf),
@@ -750,9 +772,10 @@
             pltpu.VMEM((STEPS, 4, 2, KEYS, ROWS), bf),
             pltpu.VMEM((3, 2 * DIM, ROWS), bf),
             pltpu.VMEM((3, 2 * DIM, ROWS), bf),
-            pltpu.VMEM((2, 2 * DIM, ROWS), f32),
-            pltpu.VMEM((2 * DIM, ROWS), bf),
-            pltpu.VMEM((2 * DIM, ROWS), bf),
+            pltpu.VMEM((4, DIM, ROWS), bf),
+            pltpu.VMEM((4, DIM, ROWS), bf),
+            pltpu.VMEM((2, DIM, ROWS), bf),
+            pltpu.VMEM((2, DIM, ROWS), bf),
             pltpu.VMEM((CHUNKS, 4) + window, f32),
             pltpu.VMEM((CHUNKS, 4) + window, bf),
             pltpu.VMEM((CHUNKS, 4) + window, bf),
@@ -764,7 +787,7 @@
             pltpu.VMEM((2,) + window, f32),
             pltpu.SMEM((4, 2 * BLK), jnp.int32),
             pltpu.SMEM((4 * CHUNKS + 4,), jnp.int32),
-            pltpu.SemaphoreType.DMA((11,)),
+            pltpu.SemaphoreType.DMA((15,)),
             pltpu.SemaphoreType.DMA((count,)),
             pltpu.SemaphoreType.DMA((count,)),
         ],

time: 85.7 us -> 78.6 us (0.917)
  Pallas kernels: 84.3 us -> 77.8 us
    pallas_call x1, Pallas kernels: 82.4 us -> 76 us  [body(): pl.pallas_call(kernel, out_shape=shapes, in_specs=[pl.BlockSpec(memory_sp...]
where the time goes in v4:
time: 78.6 us; the launch traced here: 78.5 us
  Pallas kernels  77.8 us (99%)
    pallas_call x1, Pallas kernels, body(): pl.pallas_call(kernel, out_shape=shapes, in_specs=[pl.BlockSpec(memory_sp...  76 us
    pallas_call x1, Pallas kernels, body(): pl.pallas_call(hand_out, out_shape=shapes, in_specs=[pl.BlockSpec(one.sha...  1.85 us

profile of v4, /device:TPU:4, one launch (start us, length us, event | category | flops | bytes accessed | tf_op | source)
XLA Modules:
  0.0 78.5 jit_solution(5987219963291299251)
XLA Ops:
  0.6 76.0 %attention.1 = (bf16[128,1024]{1,0:T(8,128)(2,1)}, bf16[128,1024]{1,0:T(8,128)(2,1)}, bf16[128,128]{1,0:T(8,128)(2,1)}, bf16[128,128]{1,0:T(8,128)(2,1)}) custom-call(s32[4,128]{1,0:T(4,128)} %pos_ref.1, bf16[128,1024]{1,0:T(8,128)(2,1)} %bitcast.8, bf16[128,128]{1,0:T(8,128)(2,1)} %bitcast.10, bf16[128,128]{1,0:T(8,128)(2,1)} %bitcast.11, ...), custom_call_target="tpu_custom_call" | custom-call | tf_op jit(solution)/shard_map/attention/pallas_call | solution.py:746
  76.6 1.9 %hand_out.1 = (bf16[128,1024]{1,0:T(8,128)(2,1)}, bf16[128,1024]{1,0:T(8,128)(2,1)}, bf16[128,128]{1,0:T(8,128)(2,1)}, bf16[128,128]{1,0:T(8,128)(2,1)}) custom-call(bf16[128,1024]{1,0:T(8,128)(2,1)} %get-tuple-element.12.refs_0_, bf16[128,1024]{1,0:T(8,128)(2,1)} %get-tuple-element.13.refs_1_, bf16[128,128]{1,0:T(8,128)(2,1)} %get-tuple-element.14.refs_2_, ...), custom_call_target="tpu_custom_call" | custom-call | tf_op jit(solution)/shard_map/hand_out/pallas_call | solution.py:799

commit v5 on v4

--- a/solution.py
+++ b/solution.py
@@ -62,6 +62,10 @@
 
 def tn(a, b):
     return lax.dot_general(a, b, (((0,), (0,)), ((), ())), preferred_element_type=jnp.float32)
+
+
+def across(a, b):
+    return lax.dot_general(a, b, (((1,), (1,)), ((), ())), preferred_element_type=jnp.float32)
 
 
 def fold(x, op):
@@ -561,21 +565,21 @@
             return p, low, p1.astype(jnp.bfloat16), ds1, p2, ds2
 
         def products(sums, p, low, p1, ds1, p2, ds2):
-            new = []
-            for one, two in (
-                (nt(ds1, qn[p, :, high]), nt(ds2, qn[p])),
-                (nt(p1, gn[p, :, high]), nt(p2, gn[p])),
-            ):
+            news = []
+            for two in (nt(ds2, qn[p]), nt(p2, gn[p])):
                 zero = jnp.zeros((HALF, DIM), jnp.float32)
                 lows, highs = [], []
                 for w in range(8):
                     here = slice(w * HALF, (w + 1) * HALF)
-                    lows.append(one[here] + lax.select(low[w], two[here, 0:DIM], zero))
+                    lows.append(lax.select(low[w], two[here, 0:DIM], zero))
                     highs.append(lax.select(low[w], zero, two[here, high]))
-                new += [lows, highs]
+                news += [lows, highs]
+            turned = [across(qt[p, high], ds1), across(gt[p, high], p1)]
             if sums is None:
-                return new
-            return [[a + b for a, b in zip(x, y)] for x, y in zip(sums, new)]
+                return news, turned
+            old, last = sums
+            news = [[a + b for a, b in zip(x, y)] for x, y in zip(old, news)]
+            return news, [a + b for a, b in zip(last, turned)]
 
         sums, late = None, None
         now = dots(parts[0])
@@ -585,7 +589,9 @@
             if late is not None:
                 sums = products(sums, *late)
             now, late = later, done
-        sums = products(sums, *late)
+        sums, turned = products(sums, *late)
+        for kind, term in zip((0, 2), turned):
+            sums[kind] = [a + b for a, b in zip(sums[kind], windows(term.T))]
         for kind in range(4):
             for w in range(8):
                 tf[2 * i + w // 4, w % 4, kind] = sums[kind][w]

time: 78.6 us -> 79.6 us (1.013)
  Pallas kernels: 77.8 us -> 78.8 us
    pallas_call x1, Pallas kernels: 76 us -> 76.9 us  [body(): pl.pallas_call(kernel, out_shape=shapes, in_specs=[pl.BlockSpec(memory_sp...]
where the time goes in v5:
time: 79.6 us; the launch traced here: 79.4 us
  Pallas kernels  78.8 us (99%)
    pallas_call x1, Pallas kernels, body(): pl.pallas_call(kernel, out_shape=shapes, in_specs=[pl.BlockSpec(memory_sp...  76.9 us
    pallas_call x1, Pallas kernels, body(): pl.pallas_call(hand_out, out_shape=shapes, in_specs=[pl.BlockSpec(one.sha...  1.85 us

profile of v5, /device:TPU:4, one launch (start us, length us, event | category | flops | bytes accessed | tf_op | source)
XLA Modules:
  0.0 79.4 jit_solution(10861129650398094127)
XLA Ops:
  0.6 76.9 %attention.1 = (bf16[128,1024]{1,0:T(8,128)(2,1)}, bf16[128,1024]{1,0:T(8,128)(2,1)}, bf16[128,128]{1,0:T(8,128)(2,1)}, bf16[128,128]{1,0:T(8,128)(2,1)}) custom-call(s32[4,128]{1,0:T(4,128)} %pos_ref.1, bf16[128,1024]{1,0:T(8,128)(2,1)} %bitcast.8, bf16[128,128]{1,0:T(8,128)(2,1)} %bitcast.10, bf16[128,128]{1,0:T(8,128)(2,1)} %bitcast.11, ...), custom_call_target="tpu_custom_call" | custom-call | tf_op jit(solution)/shard_map/attention/pallas_call | solution.py:752
  77.6 1.9 %hand_out.1 = (bf16[128,1024]{1,0:T(8,128)(2,1)}, bf16[128,1024]{1,0:T(8,128)(2,1)}, bf16[128,128]{1,0:T(8,128)(2,1)}, bf16[128,128]{1,0:T(8,128)(2,1)}) custom-call(bf16[128,1024]{1,0:T(8,128)(2,1)} %get-tuple-element.12.refs_0_, bf16[128,1024]{1,0:T(8,128)(2,1)} %get-tuple-element.13.refs_1_, bf16[128,128]{1,0:T(8,128)(2,1)} %get-tuple-element.14.refs_2_, ...), custom_call_target="tpu_custom_call" | custom-call | tf_op jit(solution)/shard_map/hand_out/pallas_call | solution.py:805

commit v6 on v4

--- a/solution.py
+++ b/solution.py
@@ -143,9 +143,10 @@
     yp, ym = (at(xx, 1, 0), inner), (at(xx, -1, 0), inner)
     zp, zm = (at(xx, 0, 1), inner), (at(xx, 0, -1), inner)
     cp, xp, dp = (outer, mate), (beside, inner), (beside, mate)
+    yp2, zp2, zm2 = (at(xx, 2, 0), inner), (at(xx, 0, 2), inner), (at(xx, 0, -2), inner)
 
     barrier = pltpu.get_barrier_semaphore()
-    for dev in (yp, ym, zp, zm, cp, xp, dp):
+    for dev in (yp, ym, zp, zm, cp, xp, dp, yp2, zp2, zm2):
         pl.semaphore_signal(barrier, inc=1, device_id=dev, device_id_type=MESH)
 
     fetch = [
@@ -166,7 +167,7 @@
                 )
     for copy in pieces + fetch:
         copy.start()
-    pl.semaphore_wait(barrier, 7)
+    pl.semaphore_wait(barrier, 10)
 
     msgs = {}
 
@@ -197,7 +198,7 @@
             msg("%s3%d" % (name, half), dst.at[1, span], dst.at[2, span], cp)
     msg("ay1", buf.at[0, 0], buf.at[0, 1], yp)
     msg("ay2", buf.at[0, 0], buf.at[0, 2], ym)
-    msg("ay3", buf.at[0, 1], buf.at[0, 3], yp)
+    msg("ay3", buf.at[0, 0], buf.at[0, 3], yp2)
     for w in range(4):
         msg("azp%d" % w, buf.at[0, w], buf.at[AT["A-1"], w], zp)
         msg("azm%d" % w, buf.at[0, w], buf.at[AT["A+1"], w], zm)
@@ -221,8 +222,8 @@
     far = AT["B0f"]
     msg("bz1", buf.at[1, 0], buf.at[1, 1], zp)
     msg("bz2", buf.at[1, 0], buf.at[1, 2], zm)
-    msg("bz3", buf.at[1, 1], buf.at[1, 3], zp)
-    msg("bz4", buf.at[1, 2], buf.at[far, 0], zm)
+    msg("bz3", buf.at[1, 0], buf.at[1, 3], zp2)
+    msg("bz4", buf.at[1, 0], buf.at[far, 0], zm2)
     msg("bz5", buf.at[1, 3], buf.at[far, 1], zp)
     msg("bz6", buf.at[far, 0], buf.at[far, 2], zm)
     msg("bz7", buf.at[far, 1], buf.at[far, 3], zp)
@@ -274,7 +275,7 @@
     go("q20", "q21", "q1")
     for copy in pieces:
         copy.wait()
-    go("ay1", "ay2", "bz1", "bz2", "azp0", "azm0", "byp0", "bym0", "g1")
+    go("ay1", "ay2", "ay3", "bz1", "bz2", "bz3", "bz4", "azp0", "azm0", "byp0", "bym0", "g1")
     fetch[0].wait()
 
     for p, (row, column) in enumerate(
@@ -295,8 +296,12 @@
 
     fetch[1].wait()
     spread(0, mq, qn, qt)
-    got("ay1", "ay2", "bz1", "bz2")
-    go("ay3", "bz3", "bz4", "azp1", "azm1", "azp2", "azm2", "byp1", "bym1", "byp2", "bym2")
+    got("ay1", "ay2", "ay3", "bz1", "bz2", "bz3", "bz4")
+    for w in range(1, 4):
+        go("azp%d" % w, "azm%d" % w)
+    go("bz5", "bz6")
+    for w in range(1, 4):
+        go("byp%d" % w, "bym%d" % w)
     got("q1")
     spread(1, pq.at[0], qn, qt)
 
@@ -317,11 +322,13 @@
     stat[2:8] = jnp.full((6, ROWS), NEG, jnp.float32)
     ls[2:8] = jnp.zeros((6, 8, ROWS), jnp.float32)
 
-    got("ay3", "bz3", "bz4")
-    go("azp3", "azm3", "bz5", "bz6", "byp3", "bym3")
     for w in range(3):
         got("azp%d" % w, "azm%d" % w)
     go("a7a", "a8a")
+    got("azp3", "azm3")
+    go("a7b", "a8b")
+    got("bz5", "bz6")
+    go("bz7", "b9a", "b10a")
     for p in range(1, 4):
         ot[p] = jnp.zeros((2 * DIM, ROWS), jnp.float32)
     for name in ("B+1n", "B2n", "B-1f", "B2f", "A4"):
@@ -329,8 +336,6 @@
     r1[AT["A-3"], 2:4] = jnp.zeros((2, 4, HALF, DIM), jnp.bfloat16)
     r1[AT["A+3"], 0:2] = jnp.zeros((2, 4, HALF, DIM), jnp.bfloat16)
 
-    got("azp3", "azm3", "bz5", "bz6")
-    go("a7b", "a8b", "bz7", "b9a", "b10a")
     got("byp0", "byp1", "byp2", "byp3")
     go("b13")
     got("q20")
@@ -373,19 +378,19 @@
 
         @pl.when(n == 1)
         def _():
+            got("a7a", "a8a", "a7b", "a8b")
+            go("a11a", "a12a", "a11b", "a12b")
+            got("bz7")
+            go("b9b", "b10b")
             got("q21")
             go("q31", "g20", "g21")
             spread(2, pq.at[1], qn, qt)
             got("q30", "q31")
             spread(3, pq.at[2], qn, qt)
-            got("a7a", "a8a", "bz7")
-            go("b9b", "b10b")
-
-        do(2, (got, ["a7b", "a8b"]), (go, ["a11a", "a12a", "a11b", "a12b"]))
+
         do(2, (got, ["bym%d" % w for w in range(4)] + ["b10a"]), (go, ["b14a"]))
-        do(3, (got, ["b10b"]), (go, ["b14b"]))
-        do(4, (got, ["a11a", "a12a"]), (go, ["a15p", "a15m"]))
-        do(4, (got, ["g20", "g21"]), (go, ["g30", "g31"]), (got, ["a11b", "a12b"]))
+        do(3, (got, ["b10b"]), (go, ["b14b"]), (got, ["a11a", "a12a"]), (go, ["a15p", "a15m"]))
+        do(4, (got, ["a11b", "a12b", "g20", "g21"]), (go, ["g30", "g31"]))
         do(6, (got, ["b14a", "b14b", "b9a", "b9b", "b13", "a15p", "a15m"]))
 
         @pl.when(n == 5)

time: 78.6 us -> 79.3 us (level)
  no operation moved by 1% of the time
where the time goes in v6:
time: 79.3 us; the launch traced here: 79.1 us
  Pallas kernels  78.5 us (99%)
    pallas_call x1, Pallas kernels, body(): pl.pallas_call(kernel, out_shape=shapes, in_specs=[pl.BlockSpec(memory_sp...  76.6 us
    pallas_call x1, Pallas kernels, body(): pl.pallas_call(hand_out, out_shape=shapes, in_specs=[pl.BlockSpec(one.sha...  1.85 us

profile of v6, /device:TPU:4, one launch (start us, length us, event | category | flops | bytes accessed | tf_op | source)
XLA Modules:
  0.0 79.1 jit_solution(15170017137585820145)
XLA Ops:
  0.6 76.6 %attention.1 = (bf16[128,1024]{1,0:T(8,128)(2,1)}, bf16[128,1024]{1,0:T(8,128)(2,1)}, bf16[128,128]{1,0:T(8,128)(2,1)}, bf16[128,128]{1,0:T(8,128)(2,1)}) custom-call(s32[4,128]{1,0:T(4,128)} %pos_ref.1, bf16[128,1024]{1,0:T(8,128)(2,1)} %bitcast.8, bf16[128,128]{1,0:T(8,128)(2,1)} %bitcast.10, bf16[128,128]{1,0:T(8,128)(2,1)} %bitcast.11, ...), custom_call_target="tpu_custom_call" | custom-call | tf_op jit(solution)/shard_map/attention/pallas_call | solution.py:751
  77.3 1.9 %hand_out.1 = (bf16[128,1024]{1,0:T(8,128)(2,1)}, bf16[128,1024]{1,0:T(8,128)(2,1)}, bf16[128,128]{1,0:T(8,128)(2,1)}, bf16[128,128]{1,0:T(8,128)(2,1)}) custom-call(bf16[128,1024]{1,0:T(8,128)(2,1)} %get-tuple-element.12.refs_0_, bf16[128,1024]{1,0:T(8,128)(2,1)} %get-tuple-element.13.refs_1_, bf16[128,128]{1,0:T(8,128)(2,1)} %get-tuple-element.14.refs_2_, ...), custom_call_target="tpu_custom_call" | custom-call | tf_op jit(solution)/shard_map/hand_out/pallas_call | solution.py:804

commit v7 on v4

--- a/solution.py
+++ b/solution.py
@@ -534,23 +534,27 @@
             parts.append((p, low, cat(vl, vh, low)))
 
         def dots(part):
-            p, _, vcat = part
-            return nt(vl, gt[p, high]), windows(nt(vcat, gt[p]))
-
-        def work(part, g1, g2):
+            p, low, vcat = part
+            el, eh = lse[8 + 2 * p : 9 + 2 * p], lse[9 + 2 * p : 10 + 2 * p]
+            first = (nt(vl, gt[p, high]) - eh).astype(jnp.bfloat16)
+            second = [
+                (dot - lax.select(pick, el, eh)).astype(jnp.bfloat16)
+                for pick, dot in zip(low, windows(nt(vcat, gt[p])))
+            ]
+            return first, second
+
+        def work(part, first, second):
             p, low, _ = part
             rl, rh = 2 * p, 2 * p + 1
-            el, eh = lse[8 + rl : 9 + rl], lse[8 + rh : 9 + rh]
             fl = jnp.exp2((mc[step, rl : rl + 1] - lse[rl : rl + 1]) * C2)
             fh = jnp.exp2((mc[step, rh : rh + 1] - lse[rh : rh + 1]) * C2)
-            p1 = wt[step, p, 0, rows].astype(jnp.float32) * fh
-            ds1 = (p1 * (g1 - eh)).astype(jnp.bfloat16)
-            w2 = windows(wt[step, p, 1, rows].astype(jnp.float32))
+            p1 = wt[step, p, 0, rows] * fh.astype(jnp.bfloat16)
+            ds1 = p1 * first
             ps, ds = [], []
-            for w in range(8):
-                piece = w2[w] * lax.select(low[w], fl, fh)
-                ps.append(piece.astype(jnp.bfloat16))
-                ds.append((piece * (g2[w] - lax.select(low[w], el, eh))).astype(jnp.bfloat16))
+            for weight, dot, pick in zip(windows(wt[step, p, 1, rows]), second, low):
+                piece = weight * lax.select(pick, fl, fh).astype(jnp.bfloat16)
+                ps.append(piece)
+                ds.append(piece * dot)
             p2, ds2 = jnp.concatenate(ps, axis=0), jnp.concatenate(ds, axis=0)
             if p < 2:
                 wt[step, p, 0, rows], wt[step, p, 1, rows] = ds1, ds2
@@ -558,7 +562,7 @@
                 one, two = tn(kl, ds1), tn(cat(kl, kh, low), ds2)
                 dqt[p, 0:DIM] = dqt[p, 0:DIM] + two[0:DIM]
                 dqt[p, high] = dqt[p, high] + (one + two[high])
-            return p, low, p1.astype(jnp.bfloat16), ds1, p2, ds2
+            return p, low, p1, ds1, p2, ds2
 
         def products(sums, p, low, p1, ds1, p2, ds2):
             new = []
@@ -728,8 +732,18 @@
 
 
 def hand_out(*refs):
-    for source, target in zip(refs[:4], refs[4:]):
-        target[...] = source[...]
+    sources, targets, held, sems = refs[:4], refs[4:8], refs[8:12], refs[12]
+    come, leave = [], []
+    for n in range(4):
+        come.append(pltpu.make_async_copy(sources[n], held[n], sems.at[n]))
+        leave.append(pltpu.make_async_copy(held[n], targets[n], sems.at[4 + n]))
+    for copy in come:
+        copy.start()
+    for first, then in zip(come, leave):
+        first.wait()
+        then.start()
+    for copy in leave:
+        copy.wait()
 
 
 def body(queries, keys, values, grad_out, block_pos):
@@ -799,9 +813,10 @@
     outs = pl.pallas_call(
         hand_out,
         out_shape=shapes,
-        in_specs=[pl.BlockSpec(one.shape, lambda n: (0, 0)) for one in shapes],
-        out_specs=[pl.BlockSpec(one.shape, lambda n: (0, 0)) for one in shapes],
-        grid=(1,),
+        in_specs=[pl.BlockSpec(memory_space=pltpu.HBM)] * 4,
+        out_specs=[pl.BlockSpec(memory_space=pltpu.HBM)] * 4,
+        scratch_shapes=[pltpu.VMEM(one.shape, bf) for one in shapes]
+        + [pltpu.SemaphoreType.DMA((8,))],
         compiler_params=pltpu.CompilerParams(vmem_limit_bytes=54 * 1024 * 1024),
         name="hand_out",
     )(*outs)

time: 78.6 us -> 77.6 us (0.987)
  Pallas kernels: 77.8 us -> 76.5 us
    pallas_call x1, Pallas kernels: 76 us -> 74.6 us  [body(): pl.pallas_call(kernel, out_shape=shapes, in_specs=[pl.BlockSpec(memory_sp...]
where the time goes in v7:
time: 77.6 us; the launch traced here: 77.1 us
  Pallas kernels  76.5 us (99%)
    pallas_call x1, Pallas kernels, body(): pl.pallas_call(kernel, out_shape=shapes, in_specs=[pl.BlockSpec(memory_sp...  74.6 us
    pallas_call x1, Pallas kernels, body(): pl.pallas_call(hand_out, out_shape=shapes, in_specs=[pl.BlockSpec(memory_...  1.82 us

profile of v7, /device:TPU:4, one launch (start us, length us, event | category | flops | bytes accessed | tf_op | source)
XLA Modules:
  0.0 77.1 jit_solution(16355987528639300584)
XLA Ops:
  0.6 74.6 %attention.1 = (bf16[128,1024]{1,0:T(8,128)(2,1)}, bf16[128,1024]{1,0:T(8,128)(2,1)}, bf16[128,128]{1,0:T(8,128)(2,1)}, bf16[128,128]{1,0:T(8,128)(2,1)}) custom-call(s32[4,128]{1,0:T(4,128)} %pos_ref.1, bf16[128,1024]{1,0:T(8,128)(2,1)} %bitcast.8, bf16[128,128]{1,0:T(8,128)(2,1)} %bitcast.10, bf16[128,128]{1,0:T(8,128)(2,1)} %bitcast.11, ...), custom_call_target="tpu_custom_call" | custom-call | tf_op jit(solution)/shard_map/attention/pallas_call | solution.py:760
  75.3 1.8 %hand_out.1 = (bf16[128,1024]{1,0:T(8,128)(2,1)}, bf16[128,1024]{1,0:T(8,128)(2,1)}, bf16[128,128]{1,0:T(8,128)(2,1)}, bf16[128,128]{1,0:T(8,128)(2,1)}) custom-call(bf16[128,1024]{1,0:T(8,128)(2,1)} %get-tuple-element.12.refs_0_, bf16[128,1024]{1,0:T(8,128)(2,1)} %get-tuple-element.13.refs_1_, bf16[128,128]{1,0:T(8,128)(2,1)} %get-tuple-element.14.refs_2_, ...), custom_call_target="tpu_custom_call" | custom-call | tf_op jit(solution)/shard_map/hand_out/pallas_call | solution.py:813

commit v8 on v7

--- a/solution.py
+++ b/solution.py
@@ -524,12 +524,11 @@
         sy[leaving] = a_total(w, *arrived).astype(jnp.bfloat16)
         go("ry%d" % leaving)
 
-    def backward(n, carry):
-        i = BACK_STEPS - 1 - n
+    def sweep(i, group, more):
         step, rows = i // 2, pl.ds((i % 2) * BACK_KEYS, BACK_KEYS)
         kl, kh, vl, vh = [take(2 * i, 2, kind) for kind in range(4)]
         parts = []
-        for p in range(4):
+        for p in group:
             low, same = picks(2 * i, 2, p)
             parts.append((p, low, cat(vl, vh, low)))
 
@@ -583,8 +582,8 @@
 
         sums, late = None, None
         now = dots(parts[0])
-        for k in range(4):
-            later = dots(parts[k + 1]) if k < 3 else None
+        for k in range(len(parts)):
+            later = dots(parts[k + 1]) if k < len(parts) - 1 else None
             done = work(parts[k], *now)
             if late is not None:
                 sums = products(sums, *late)
@@ -592,7 +591,13 @@
         sums = products(sums, *late)
         for kind in range(4):
             for w in range(8):
-                tf[2 * i + w // 4, w % 4, kind] = sums[kind][w]
+                c = 2 * i + w // 4
+                term = sums[kind][w]
+                tf[c, w % 4, kind] = tf[c, w % 4, kind] + term if more else term
+
+    def backward(n, carry):
+        i = BACK_STEPS - 1 - n
+        sweep(i, range(4), False)
 
         def finish(at_step, *chunks):
             @pl.when(i == at_step)
@@ -631,7 +636,18 @@
 
         return carry
 
-    lax.fori_loop(0, BACK_STEPS, backward, 0)
+    lax.fori_loop(0, BACK_STEPS - 1, backward, 0)
+
+    sweep(0, (2, 3), False)
+    for lh in range(2):
+        sd[lh] = dqt[3, lh * DIM : (lh + 1) * DIM].astype(jnp.bfloat16)
+        go("dq3%d" % lh)
+    sweep(0, (0, 1), True)
+    for lh in range(2):
+        got("dq3%d" % lh)
+        part = dqt[2, lh * DIM : (lh + 1) * DIM] + pd[lh].astype(jnp.float32)
+        xd[lh] = part.astype(jnp.bfloat16)
+        go("dq2%d" % lh)
 
     def store(ref, rows):
         for h in range(HEADS):
@@ -657,19 +673,11 @@
             halves.append(total)
         store(att_ref, jnp.concatenate(halves, axis=0).T.astype(jnp.bfloat16))
 
-    for lh in range(2):
-        sd[lh] = dqt[3, lh * DIM : (lh + 1) * DIM].astype(jnp.bfloat16)
-        go("dq3%d" % lh)
     got("rB-1n0", "rB-1n1", "rB+1n0", "rB+1n1")
     chain(-2, 2, 1)
     chain(1, 6, 5)
     attend()
     leave[0].start()
-    for lh in range(2):
-        got("dq3%d" % lh)
-        part = dqt[2, lh * DIM : (lh + 1) * DIM] + pd[lh].astype(jnp.float32)
-        xd[lh] = part.astype(jnp.bfloat16)
-        go("dq2%d" % lh)
 
     def queries_back(n, carry):
         def stage(at_step):

time: 77.6 us -> 77.7 us (level); the launches traced: 77.1 us -> 76.4 us
  Pallas kernels: 76.5 us -> 75.7 us
where the time goes in v8:
time: 77.7 us; the launch traced here: 76.4 us
  Pallas kernels  75.7 us (97%)
    pallas_call x1, Pallas kernels, body(): pl.pallas_call(kernel, out_shape=shapes, in_specs=[pl.BlockSpec(memory_sp...  73.9 us
    pallas_call x1, Pallas kernels, body(): pl.pallas_call(hand_out, out_shape=shapes, in_specs=[pl.BlockSpec(memory_...  1.82 us

profile of v8, /device:TPU:4, one launch (start us, length us, event | category | flops | bytes accessed | tf_op | source)
XLA Modules:
  0.0 76.4 jit_solution(4772640997769632733)
XLA Ops:
  0.6 73.9 %attention.1 = (bf16[128,1024]{1,0:T(8,128)(2,1)}, bf16[128,1024]{1,0:T(8,128)(2,1)}, bf16[128,128]{1,0:T(8,128)(2,1)}, bf16[128,128]{1,0:T(8,128)(2,1)}) custom-call(s32[4,128]{1,0:T(4,128)} %pos_ref.1, bf16[128,1024]{1,0:T(8,128)(2,1)} %bitcast.8, bf16[128,128]{1,0:T(8,128)(2,1)} %bitcast.10, bf16[128,128]{1,0:T(8,128)(2,1)} %bitcast.11, ...), custom_call_target="tpu_custom_call" | custom-call | tf_op jit(solution)/shard_map/attention/pallas_call | solution.py:768
  74.5 1.8 %hand_out.1 = (bf16[128,1024]{1,0:T(8,128)(2,1)}, bf16[128,1024]{1,0:T(8,128)(2,1)}, bf16[128,128]{1,0:T(8,128)(2,1)}, bf16[128,128]{1,0:T(8,128)(2,1)}) custom-call(bf16[128,1024]{1,0:T(8,128)(2,1)} %get-tuple-element.12.refs_0_, bf16[128,1024]{1,0:T(8,128)(2,1)} %get-tuple-element.13.refs_1_, bf16[128,128]{1,0:T(8,128)(2,1)} %get-tuple-element.14.refs_2_, ...), custom_call_target="tpu_custom_call" | custom-call | tf_op jit(solution)/shard_map/hand_out/pallas_call | solution.py:821
